TPU v7x, 256 devices: a whole 4x4x8 slice. The times are simulated.
256 devices in a mesh: rep: 8 (over x, z_hi), ep: 32 (over y, z_lo, core).
Axes of the slice: x: 4, y: 4, z: 8 (z_hi: 2, z_lo: 4; z = z_hi * 4 + z_lo), core: 2. Of those that a mesh axis runs over, the one named last changes fastest.
Arguments:
- tokens: bfloat16 [5120, 7168], P('ep', 'rep'), may hold values from -6 to 6
- slot_ids: int32 [5120, 2], P('ep'), may hold values from 0 to 63, all different within a row; in each aligned block of 160 rows (0 to 159, 160 to 319, ...) at most 10 rows name the same one
- gate_weights_per_slot: float32 [5120, 2], P('ep'), may hold values from 0.1 to 1
- w_gate: bfloat16 [32, 7168, 2048], P('ep', None, 'rep'), may hold values from -0.0625 to 0.0625
- w_up: bfloat16 [32, 7168, 2048], P('ep', None, 'rep'), may hold values from -0.0625 to 0.0625
- w_down: bfloat16 [32, 2048, 7168], P('ep', 'rep'), may hold values from -0.1875 to 0.1875
Outputs:
- moe_output: bfloat16 [5120, 7168], P('ep', 'rep')
Inputs may be any that keep to these rules, and one draw needn't show every extreme that they name: `slot_ids`: in each aligned block of 160 rows (the tokens of one index of ep) no slot is named by more than 10 rows, a bound that some block reaches; the 2 slots of a row differ.
All inputs are finite; a program needn't handle non-finite values.
Results may differ from a plain program's by a relative error of at most 0.017.
Values may be sent and summed in bfloat16 or wider, within the bound.
No kernel may reach another device: no remote copies, remote signals or barrier semaphores. Data moves between devices by JAX's collectives and lax.ppermute only.
A program may use at most 128 MiB of HBM per device.

v0:
```python
import jax
import jax.numpy as jnp
from jax import lax
from jax.sharding import PartitionSpec as P


def shifted(x, axis, by):
    length = lax.axis_size(axis)
    return lax.ppermute(x, axis, [(i, (i + by) % length) for i in range(length)])


def slot_targets(slot_ids, n_ep, capacity):
    flattened = slot_ids.reshape(-1)
    onehot = (flattened[:, None] == jnp.arange(2 * n_ep, dtype=jnp.int32)[None, :]).astype(
        jnp.int32
    )
    position = jnp.sum((jnp.cumsum(onehot, axis=0) - onehot) * onehot, axis=1)
    return flattened % 2 * (n_ep * capacity) + flattened // 2 * capacity + position


def pack_rows(source, targets, top_count, n_ep, capacity):
    copies = jnp.repeat(source, top_count, axis=0)
    buffer = jnp.zeros((2 * n_ep * capacity, source.shape[1]), source.dtype).at[targets].set(copies)
    return buffer.reshape(2, n_ep, capacity, source.shape[1])


def expert_terms(arrived, gate_mat, up_weight_matrix, down_mat):
    inputs = arrived.reshape(-1, arrived.shape[-1])
    gate_val = jnp.dot(inputs, gate_mat, preferred_element_type=jnp.float32)
    up_val = jnp.dot(inputs, up_weight_matrix, preferred_element_type=jnp.float32)
    hidden_state = (jax.nn.silu(gate_val) * up_val).astype(jnp.bfloat16)
    return jnp.dot(hidden_state, down_mat, preferred_element_type=jnp.float32)


def shards(tokens, slot_ids, gate_weights_per_slot, w_gate, w_up, w_down):
    n_ep = lax.axis_size("ep")
    capacity = tokens.shape[0] // 16
    top_count = slot_ids.shape[1]
    spare_gate, spare_up, spare_down = shifted((w_gate, w_up, w_down), "ep", 1)
    targets = slot_targets(slot_ids, n_ep, capacity)
    wide_tokens = lax.all_gather(tokens, "rep", axis=1, tiled=True)
    arrived = lax.all_to_all(
        pack_rows(wide_tokens, targets, top_count, n_ep, capacity),
        "ep",
        split_axis=1,
        concat_axis=1,
        tiled=True,
    )
    home_rows = arrived[0]
    copy_rows = arrived[1]
    home_terms = expert_terms(home_rows, w_gate[0], w_up[0], w_down[0])
    copy_terms = expert_terms(copy_rows, spare_gate[0], spare_up[0], spare_down[0])
    paired_terms = jnp.stack([home_terms, copy_terms])
    rounded = lax.optimization_barrier(paired_terms.astype(jnp.bfloat16)).astype(jnp.float32)
    summed = lax.psum_scatter(rounded.astype(jnp.bfloat16), "rep", scatter_dimension=2, tiled=True)
    slice_width = summed.shape[2]
    returned = lax.all_to_all(
        summed.reshape(2, n_ep, capacity, slice_width),
        "ep",
        split_axis=1,
        concat_axis=1,
        tiled=True,
    )
    selected_rows = returned.reshape(-1, slice_width)[targets].astype(jnp.float32)
    selected_rows = selected_rows.reshape(tokens.shape[0], top_count, slice_width)
    combined = jnp.sum(gate_weights_per_slot[:, :, None] * selected_rows, axis=1)
    return combined.astype(jnp.bfloat16)


def solution(mesh):
    placed = (
        P("ep", "rep"),
        P("ep", None),
        P("ep", None),
        P("ep", None, "rep"),
        P("ep", None, "rep"),
        P("ep", "rep", None),
    )
    return jax.shard_map(
        shards, mesh=mesh, in_specs=placed, out_specs=P("ep", "rep"), check_vma=False
    )
```

profile of v0, /device:TPU:1, one launch (start us, length us, event | category | flops | bytes accessed | tf_op | source)
XLA Modules:
  0.0 924.7 jit_solution(9746078309753942761)
XLA Ops:
  6.5 0.7 all-gather.2.cloned.1.call-update
  7.3 0.8 copy.16
  8.0 0.1 eq.24
  8.2 0.1 reshape.152
  8.4 0.9 reduce-window.6
  9.3 0.2 slice_reduce_fusion.2
  9.5 0.1 bitcast_bitcast_fusion
  9.7 79.8 %all-gather.2.cloned.1.call-done = bf16[160,7168]{1,0:T(8,128)(2,1)} async-done(((bf16[160,896]{1,0:T(8,128)(2,1)}), bf16[160,7168]{1,0:T(8,128)(2,1)}) %all-gather.2.cloned.1.call-update) | async-done | bytes 2293776 | tf_op jit(solution)/shard_map/all_gather | solution.py:41
  89.6 6.6 broadcast_in_dim.5
  96.2 7.5 reshape.173
  103.7 13.9 %scatter_custom_fusion = bf16[640,7168]{1,0:T(8,128)(2,1)} fusion(s32[320]{0:T(512)S(1)} %fusion.23, bf16[320,7168]{1,0:T(8,128)(2,1)} %reshape.173, bf16[]{:T(256)} %constant.37.clone.1), kind=kCustom, calls=%fused_computation.9 | custom fusion | bytes 9175552 | tf_op jit(solution)/shard_map/scatter | solution.py:23
  117.6 14.4 %reshape.156 = bf16[2,32,10,7168]{3,2,1,0:T(8,128)(2,1)} reshape(bf16[640,7168]{1,0:T(8,128)(2,1)} %scatter_custom_fusion) | data formatting | bytes 18350080 | tf_op jit(solution)/shard_map/reshape | solution.py:24
  132.0 17.9 %copy.20 = bf16[2,32,10,7168]{3,0,2,1:T(2,128)(2,1)} copy(bf16[2,32,10,7168]{3,2,1,0:T(8,128)(2,1)} %reshape.156) | data formatting | bytes 18350080 | tf_op jit(solution)/shard_map/reshape | solution.py:24
  149.9 8.1 all-to-all-start
  158.0 0.0 reduce-scatter.4.cloned.1.call-start
  158.0 1.7 collective-permute-start.1
  159.7 0.1 collective-permute-start
  159.9 1.6 collective-permute-start.2
  161.4 315.7 %all-to-all-done = bf16[2,32,10,7168]{3,0,2,1:T(2,128)(2,1)} async-done(((bf16[2,32,10,7168]{3,0,2,1:T(2,128)(2,1)}), bf16[2,32,10,7168]{3,0,2,1:T(2,128)(2,1)}, u32[]{:S(2)}, u32[]{:S(2)}) %all-to-all-start) | async-done | bytes 9175072 | tf_op jit(solution)/shard_map/all_to_all | solution.py:42
  477.2 102.8 %slice_reduce_fusion.1 = (bf16[32,10,7168]{2,1,0:T(8,128)(2,1)}, bf16[32,10,7168]{2,1,0:T(8,128)(2,1)}) fusion(bf16[2,32,10,7168]{3,0,2,1:T(2,128)(2,1)} %all-to-all-done), kind=kLoop, calls=%fused_computation.5 | loop fusion | bytes 18350080 | tf_op jit(solution)/shard_map/slice | solution.py:49
  580.0 8.1 reshape_squeeze.6
  588.0 8.3 reshape_squeeze.7
  596.4 0.0 slice-start.3
  596.4 0.0 copy-start.2
  596.4 4.9 fusion.12
  601.4 0.8 copy-done.2
  602.1 1.3 fusion.17
  603.5 0.9 copy-done
  604.3 3.4 fusion
  607.8 3.4 fusion.5
  611.2 3.4 fusion.7
  614.6 5.6 fusion.1
  620.1 8.0 pad_maximum_fusion
  628.2 27.5 %copy.23 = bf16[2,320,7168]{1,0,2:T(2,128)(2,1)} copy(bf16[2,320,7168]{2,1,0:T(8,128)(2,1)} %pad_maximum_fusion) | data formatting | bytes 18350080
  655.7 21.8 %reshape.177 = bf16[7168,640]{1,0:T(8,128)(2,1)} reshape(bf16[7168,2,320]{2,1,0:T(2,128)(2,1)} %bitcast.47) | data formatting | bytes 18350080
  677.5 0.0 reduce-scatter.4.cloned.1.call-update
  677.5 0.0 copy-start.1
  677.5 188.6 %reduce-scatter.4.cloned.1.call-done = bf16[896,640]{1,0:T(8,128)(2,1)} async-done(((bf16[7168,640]{1,0:T(8,128)(2,1)}), bf16[896,640]{1,0:T(8,128)(2,1)}) %reduce-scatter.4.cloned.1.call-update) | async-done | bytes 1146896
  866.1 3.4 reshape.178
  869.5 3.6 copy.21
  873.1 9.0 all-to-all-start.1
  882.1 0.1 copy.15
  882.3 29.7 %all-to-all-done.1 = bf16[2,32,10,896]{3,0,2,1:T(2,128)(2,1)S(1)} async-done(((bf16[2,32,10,896]{3,0,2,1:T(2,128)(2,1)}), bf16[2,32,10,896]{3,0,2,1:T(2,128)(2,1)S(1)}, u32[]{:S(2)}, u32[]{:S(2)}) %all-to-all-start.1) | async-done | bytes 1146912 | tf_op jit(solution)/shard_map/all_to_all | solution.py:57
  911.9 0.2 copy.22
  912.2 0.4 reshape.158
  912.6 2.2 gather_fusion
  914.8 0.6 reshape.160
  915.4 2.2 multiply_reduce_fusion
  (21 shorter events, 0.2 us)
Async XLA Ops:
  6.5 83.0 %all-gather.2.cloned.1.call-start = ((), (), s32[]{:S(2)}) async-start(), calls=%async_computation.3 | async-start | bytes 2580480 | tf_op jit(solution)/shard_map/all_gather | solution.py:41
  149.9 327.3 %all-to-all-start = ((bf16[2,32,10,7168]{3,0,2,1:T(2,128)(2,1)}), bf16[2,32,10,7168]{3,0,2,1:T(2,128)(2,1)}, u32[]{:S(2)}, u32[]{:S(2)}) async-start(bf16[2,32,10,7168]{3,0,2,1:T(2,128)(2,1)} %copy.20), calls=%async_computation | async-start | bytes 18350080 | tf_op jit(solution)/shard_map/all_to_all | solution.py:42
  158.0 708.1 %reduce-scatter.4.cloned.1.call-start = ((), (), s32[]{:S(2)}) async-start(), calls=%async_computation.4 | async-start | bytes 10321920
  158.0 449.8 %collective-permute-start.1 = (bf16[1,7168,256]{2,1,0:T(8,128)(2,1)}, bf16[1,7168,256]{2,1,0:T(8,128)(2,1)}, u32[]{:S(2)}, u32[]{:S(2)}) collective-permute-start(bf16[1,7168,256]{2,1,0:T(8,128)(2,1)} %param.10), channel_id=1, source_target_pairs={{0,1},{1,2},{2,3},{3,4},{4,5},{5,6},{6,7},{7,8},{8,9},{9,10},{10,1... | collective-permute-start | bytes 11010056 | tf_op jit(solution)/shard_map/ppermute | solution.py:9
  159.7 451.5 %collective-permute-start = (bf16[1,7168,256]{2,1,0:T(8,128)(2,1)}, bf16[1,7168,256]{2,1,0:T(8,128)(2,1)}, u32[]{:S(2)}, u32[]{:S(2)}) collective-permute-start(bf16[1,7168,256]{2,1,0:T(8,128)(2,1)} %param.9), channel_id=1, source_target_pairs={{0,1},{1,2},{2,3},{3,4},{4,5},{5,6},{6,7},{7,8},{8,9},{9,10},{10,1... | collective-permute-start | bytes 11010056 | tf_op jit(solution)/shard_map/ppermute | solution.py:9
  159.9 454.7 %collective-permute-start.2 = (bf16[1,256,7168]{2,1,0:T(8,128)(2,1)}, bf16[1,256,7168]{2,1,0:T(8,128)(2,1)}, u32[]{:S(2)}, u32[]{:S(2)}) collective-permute-start(bf16[1,256,7168]{2,1,0:T(8,128)(2,1)} %param.11), channel_id=1, source_target_pairs={{0,1},{1,2},{2,3},{3,4},{4,5},{5,6},{6,7},{7,8},{8,9},{9,10},{10,1... | collective-permute-start | bytes 11010056 | tf_op jit(solution)/shard_map/ppermute | solution.py:9
  588.0 13.3 %slice-start.2 = ((s8[4587520]{0:T(1024)(128)(4,1)}), s8[393216]{0:T(1024)(128)(4,1)S(1)}, s32[]{:S(2)}) async-start(s8[4587520]{0:T(1024)(128)(4,1)} %bitcast.51), calls=%async_computation.7 | async-start | bytes 786432
  596.4 5.0 slice-start.3
  596.4 5.7 copy-start.2
  596.4 11.4 %slice-start = ((s8[4587520]{0:T(1024)(128)(4,1)}), s8[4194304]{0:T(1024)(128)(4,1)S(1)}, s32[]{:S(2)}) async-start(s8[4587520]{0:T(1024)(128)(4,1)} %bitcast.49), calls=%async_computation.5 | async-start | bytes 8388608
  602.1 2.2 copy-start
  602.1 5.6 slice-start.1
  677.5 204.6 %copy-start.1 = (f32[160,2]{0,1:T(2,128)S(1)}, f32[160,2]{0,1:T(2,128)}, u32[]{:S(2)}) copy-start(f32[160,2]{0,1:T(2,128)} %param.8) | copy-start | bytes 3844
  873.1 38.8 %all-to-all-start.1 = ((bf16[2,32,10,896]{3,0,2,1:T(2,128)(2,1)}), bf16[2,32,10,896]{3,0,2,1:T(2,128)(2,1)S(1)}, u32[]{:S(2)}, u32[]{:S(2)}) async-start(bf16[2,32,10,896]{3,0,2,1:T(2,128)(2,1)} %bitcast.9), calls=%async_computation.1 | async-start | bytes 2293760 | tf_op jit(solution)/shard_map/all_to_all | solution.py:57
Sparse Core Ops, SparseCore 0:
  10.0 79.5 all-gather.1
  677.6 188.4 reduce-scatter.3
where the time goes:
time: 934 us; the launch traced here: 925 us
  waiting for transfers between devices  615 us (66%)
  local copies, waits for them, and re-layouts  242 us (26%)
  matrix products  22 us (2%)
  starting transfers between devices  20.6 us (2%)
  between operations  13.9 us (1%)
  other arithmetic  11.3 us (1%)
    all_to_all x1, waiting for transfers between devices, shards(): lax.all_to_all(pack_rows(wide_tokens, targets, top_count, n_ep, capacity)...  316 us
    unnamed x3, waiting for transfers between devices  189 us
    slice x1, local copies, waits for them, and re-layouts, shards(): home_rows = arrived[0]  103 us
    all_gather x1, waiting for transfers between devices, shards(): wide_tokens = lax.all_gather(tokens, 'rep', axis=1, tiled=True)  79.8 us
    unnamed x19, local copies, waits for them, and re-layouts  55.2 us
    reshape x2, local copies, waits for them, and re-layouts, pack_rows(): return buffer.reshape(2, n_ep, capacity, source.shape[1])  32.3 us
    all_to_all x1, waiting for transfers between devices, shards(): lax.all_to_all(summed.reshape(2, n_ep, capacity, slice_width), 'ep', spli...  29.7 us
  transfers between devices with their start and end apart: 7, of which 4 were waited for; matrix products, arithmetic and copies ran while one was open for 15% of the time, Pallas kernels for 0%

commit v1 on v0

v1 whole, which is shorter than its diff:
```python
import functools

import jax
import jax.numpy as jnp
from jax import lax
from jax.experimental import pallas as pl
from jax.experimental.pallas import tpu as pltpu
from jax.sharding import PartitionSpec as P

CAP_PAIR = 20
PAD_PAIR = 24
ROW_TILE = 160


def move(x, by):
    return lax.ppermute(x, "rep", [(i, (i + 2 * by) % 8) for i in range(8)])


def swap(x):
    return lax.ppermute(x, "rep", [(i, i ^ 1) for i in range(8)])


def place_rows(slot_ids, n_ep):
    flat = slot_ids.T.reshape(-1)
    count = flat.shape[0]
    onehot = (flat[:, None] == jnp.arange(2 * n_ep, dtype=jnp.int32)[None, :]).astype(jnp.bfloat16)
    before = jnp.tril(jnp.ones((count, count), jnp.bfloat16), -1)
    ahead = jnp.dot(before, onehot, preferred_element_type=jnp.float32)
    position = jnp.sum(ahead * onehot.astype(jnp.float32), axis=1).astype(jnp.int32)
    odd = flat % 2
    expert = (flat // 2 - odd + n_ep) % n_ep
    row = expert * PAD_PAIR + odd * (CAP_PAIR // 2) + position
    return row.reshape(2, -1)


def exchange(rows, n_ep):
    width = rows.shape[1]
    out = lax.all_to_all(rows.reshape(n_ep, PAD_PAIR, width), "ep", 0, 0, tiled=True)
    return out.reshape(n_ep * PAD_PAIR, width)


def compact_matrix(n_ep):
    r = lax.broadcasted_iota(jnp.int32, (n_ep * CAP_PAIR, n_ep * PAD_PAIR), 0)
    c = lax.broadcasted_iota(jnp.int32, (n_ep * CAP_PAIR, n_ep * PAD_PAIR), 1)
    return (r // CAP_PAIR * PAD_PAIR + r % CAP_PAIR == c).astype(jnp.bfloat16)


def pick(matrix, rows):
    return jnp.dot(matrix, rows, preferred_element_type=jnp.float32).astype(jnp.bfloat16)


def gather_x(mine):
    half = mine.shape[0] // 2
    left = move(mine, 1)
    right = move(mine, -1)
    top = move(left[:half], 1)
    bottom = move(right[half:], -1)
    return [mine, right, jnp.concatenate([top, bottom], axis=0), left]


def add(a, b):
    return (a.astype(jnp.float32) + b.astype(jnp.float32)).astype(jnp.bfloat16)


def reduce_x(parts):
    half = parts[0].shape[0] // 2
    top = move(parts[2][:half], 1)
    bottom = move(parts[2][half:], -1)
    one = jnp.concatenate([add(parts[1][:half], top), parts[1][half:]], axis=0)
    three = jnp.concatenate([parts[3][:half], add(parts[3][half:], bottom)], axis=0)
    from_left = move(one, 1)
    from_right = move(three, -1)
    total = parts[0].astype(jnp.float32) + from_left.astype(jnp.float32)
    return (total + from_right.astype(jnp.float32)).astype(jnp.bfloat16)


def first_kernel(idx, *refs):
    xs, gates, ups = refs[:4], refs[4:8], refs[8:12]
    g_ref, u_ref = refs[12:]
    g_ref[...] = sum(
        jnp.dot(x[...], w[...], preferred_element_type=jnp.float32) for x, w in zip(xs, gates)
    )
    u_ref[...] = sum(
        jnp.dot(x[...], w[...], preferred_element_type=jnp.float32) for x, w in zip(xs, ups)
    )


def second_kernel(idx, *refs):
    g_ref, u_ref = refs[:2]
    xs, gates, ups, downs, outs = refs[2:6], refs[6:10], refs[10:14], refs[14:22], refs[22:]
    gate = g_ref[...] + sum(
        jnp.dot(x[...], w[...], preferred_element_type=jnp.float32) for x, w in zip(xs, gates)
    )
    up = u_ref[...] + sum(
        jnp.dot(x[...], w[...], preferred_element_type=jnp.float32) for x, w in zip(xs, ups)
    )
    hidden = (gate / (1.0 + jnp.exp(-gate)) * up).astype(jnp.bfloat16)
    for down, out in zip(downs, outs):
        out[...] = jnp.dot(hidden, down[...], preferred_element_type=jnp.float32).astype(
            jnp.bfloat16
        )


def rows_spec(width):
    return pl.BlockSpec((ROW_TILE, width), lambda i, idx: (i, 0))


def first_half(idx, xs, w_gate, w_up):
    rows, width = xs[0].shape
    hidden = w_gate.shape[1]
    wspecs = [pl.BlockSpec((width, hidden), lambda i, idx, d=d: (idx[d], 0)) for d in range(4)]
    return pl.pallas_call(
        first_kernel,
        grid_spec=pltpu.PrefetchScalarGridSpec(
            num_scalar_prefetch=1,
            grid=(rows // ROW_TILE,),
            in_specs=[rows_spec(width)] * 4 + wspecs * 2,
            out_specs=[rows_spec(hidden)] * 2,
        ),
        out_shape=[jax.ShapeDtypeStruct((rows, hidden), jnp.float32)] * 2,
        compiler_params=pltpu.CompilerParams(vmem_limit_bytes=40 * 2**20),
        cost_estimate=pl.CostEstimate(
            flops=16 * rows * width * hidden, bytes_accessed=20 * 2**20, transcendentals=0
        ),
    )(idx, *xs, *[w_gate] * 4, *[w_up] * 4)


def second_half(idx, sums, xs, w_gate, w_up, w_down):
    rows, width = xs[0].shape
    hidden = w_gate.shape[1]
    wspecs = [pl.BlockSpec((width, hidden), lambda i, idx, d=d: (idx[4 + d], 0)) for d in range(4)]
    dspecs = [pl.BlockSpec((hidden, width), lambda i, idx, d=d: (0, idx[d])) for d in range(8)]
    return pl.pallas_call(
        second_kernel,
        grid_spec=pltpu.PrefetchScalarGridSpec(
            num_scalar_prefetch=1,
            grid=(rows // ROW_TILE,),
            in_specs=[rows_spec(hidden)] * 2 + [rows_spec(width)] * 4 + wspecs * 2 + dspecs,
            out_specs=[rows_spec(width)] * 8,
        ),
        out_shape=[jax.ShapeDtypeStruct((rows, width), jnp.bfloat16)] * 8,
        compiler_params=pltpu.CompilerParams(vmem_limit_bytes=48 * 2**20),
        cost_estimate=pl.CostEstimate(
            flops=32 * rows * width * hidden,
            bytes_accessed=30 * 2**20,
            transcendentals=rows * hidden,
        ),
    )(idx, *sums, *xs, *[w_gate] * 4, *[w_up] * 4, *[w_down] * 8)


def shards(tokens, slot_ids, weights, w_gate, w_up, w_down):
    n_ep = lax.axis_size("ep")
    rep = lax.axis_index("rep")
    x, zh = rep // 2, rep % 2
    steps = jnp.arange(4, dtype=jnp.int32)
    around = (x + steps) % 4 * 2
    idx = jnp.concatenate([around + zh, around + 1 - zh]).astype(jnp.int32)

    other_tokens = swap(tokens)
    row = place_rows(slot_ids, n_ep)
    slots = lax.broadcasted_iota(jnp.int32, (n_ep * PAD_PAIR, tokens.shape[0]), 0)
    pack = ((slots == row[0][None]) | (slots == row[1][None])).astype(jnp.bfloat16)
    compact = compact_matrix(n_ep)

    mine = pick(compact, exchange(pick(pack, tokens), n_ep))
    own = gather_x(mine)
    theirs = pick(compact, exchange(pick(pack, other_tokens), n_ep))
    other = gather_x(theirs)

    sums = first_half(idx, own, w_gate[0], w_up[0])
    terms = second_half(idx, sums, other, w_gate[0], w_up[0], w_down[0])

    spread = compact.T
    columns = lax.broadcasted_iota(jnp.int32, (tokens.shape[0], n_ep * PAD_PAIR), 1)
    choose = [(columns == row[k][:, None]).astype(jnp.bfloat16) for k in range(2)]

    def combine(rows):
        return sum(
            weights[:, k : k + 1] * jnp.dot(choose[k], rows, preferred_element_type=jnp.float32)
            for k in range(2)
        )

    back_other = exchange(pick(spread, reduce_x(terms[4:])), n_ep)
    sent = swap(combine(back_other).astype(jnp.bfloat16))
    back_own = exchange(pick(spread, reduce_x(terms[:4])), n_ep)
    return (combine(back_own) + sent.astype(jnp.float32)).astype(jnp.bfloat16)


def solution(mesh):
    placed = (
        P("ep", "rep"),
        P("ep", None),
        P("ep", None),
        P("ep", None, "rep"),
        P("ep", None, "rep"),
        P("ep", "rep", None),
    )
    return jax.shard_map(
        shards, mesh=mesh, in_specs=placed, out_specs=P("ep", "rep"), check_vma=False
    )
```

time: 934 us -> 328 us (0.35)
  waiting for transfers between devices: 615 us -> 211 us
  local copies, waits for them, and re-layouts: 242 us -> 9.77 us
  starting transfers between devices: 20.6 us -> 64.1 us
  Pallas kernels: 0 us -> 16.1 us
  between operations: 13.9 us -> 0.32 us
    all_to_all x2 -> x4, waiting for transfers between devices: 345 us -> 74.9 us  [exchange(): lax.all_to_all(rows.reshape(n_ep, PAD_PAIR, width), 'ep', 0, 0, tiled=True)]
    unnamed x3 -> x0, waiting for transfers between devices: 189 us -> none
    ppermute x3 -> x18, waiting for transfers between devices: 0.01 us -> 136 us  [the longest x16 101 us: move(): return lax.ppermute(x, 'rep', [(i, (i + 2 * by) % 8) for i in range(8)])]
    slice x2 -> x12, local copies, waits for them, and re-layouts: 103 us -> 6.95 us  [the longest x2 2.58 us: reduce_x(): top = move(parts[2][:half], 1)]
    all_gather x1 -> x0, waiting for transfers between devices: 79.8 us -> none  [shards(): wide_tokens = lax.all_gather(tokens, 'rep', axis=1, tiled=True)]
    unnamed x19 -> x14, local copies, waits for them, and re-layouts: 55.2 us -> 2.06 us
    reshape x5 -> x1, local copies, waits for them, and re-layouts: 40.4 us -> 0.76 us  [place_rows(): flat = slot_ids.T.reshape(-1)]
    ppermute x3 -> x18, starting transfers between devices: 3.44 us -> 29.4 us  [the longest x16 20.8 us: move(): return lax.ppermute(x, 'rep', [(i, (i + 2 * by) % 8) for i in range(8)])]
  transfers between devices with their start and end apart: 7 -> 22, of which waited for: 4 -> 12; matrix products, arithmetic and copies ran while one was open for 15% -> 8% of each run, Pallas kernels for 0% -> 1%
where the time goes in v1:
time: 328 us; the launch traced here: 327 us
  waiting for transfers between devices  211 us (64%)
  starting transfers between devices  64.1 us (20%)
  matrix products  21.6 us (7%)
  Pallas kernels  16.1 us (5%)
  local copies, waits for them, and re-layouts  9.77 us (3%)
  other arithmetic  4.58 us (1%)
    ppermute x16, waiting for transfers between devices, move(): return lax.ppermute(x, 'rep', [(i, (i + 2 * by) % 8) for i in range(8)])  101 us
    all_to_all x4, waiting for transfers between devices, exchange(): lax.all_to_all(rows.reshape(n_ep, PAD_PAIR, width), 'ep', 0, 0, tiled=True)  74.9 us
    ppermute x2, waiting for transfers between devices, swap(): return lax.ppermute(x, 'rep', [(i, i ^ 1) for i in range(8)])  35.4 us
    all_to_all x4, starting transfers between devices, exchange(): lax.all_to_all(rows.reshape(n_ep, PAD_PAIR, width), 'ep', 0, 0, tiled=True)  34.7 us
    ppermute x16, starting transfers between devices, move(): return lax.ppermute(x, 'rep', [(i, (i + 2 * by) % 8) for i in range(8)])  20.8 us
    dot_general x6, matrix products, pick(): jnp.dot(matrix, rows, preferred_element_type=jnp.float32)  16.1 us
    pallas_call x1, Pallas kernels, second_half(): pl.pallas_call(second_kernel, grid_spec=pltpu.PrefetchScalarGridSpec(num_...  12.1 us
    ppermute x2, starting transfers between devices, swap(): return lax.ppermute(x, 'rep', [(i, i ^ 1) for i in range(8)])  8.6 us
  transfers between devices with their start and end apart: 22, of which 12 were waited for; matrix products, arithmetic and copies ran while one was open for 8% of the time, Pallas kernels for 1%

profile of v1, /device:TPU:1, one launch (start us, length us, event | category | flops | bytes accessed | tf_op | source)
XLA Modules:
  0.0 327.5 jit_solution(15116629661954959888)
XLA Ops:
  1.2 2.6 convolution_convert_fusion.3
  3.8 10.3 %all-to-all-start = ((bf16[32,24,896]{2,1,0:T(8,128)(2,1)}), bf16[32,24,896]{2,1,0:T(8,128)(2,1)S(1)}, u32[]{:S(2)}, u32[]{:S(2)}) async-start(bf16[32,24,896]{2,1,0:T(8,128)(2,1)} %bitcast.51), calls=%async_computation | async-start | bytes 2752512 | tf_op jit(solution)/shard_map/all_to_all | solution.py:38
  14.1 4.3 %collective-permute-start.4 = (bf16[160,896]{1,0:T(8,128)(2,1)S(1)}, bf16[160,896]{1,0:T(8,128)(2,1)S(1)}, u32[]{:S(2)}, u32[]{:S(2)}) collective-permute-start(bf16[160,896]{1,0:T(8,128)(2,1)S(1)} %copy-done.6), channel_id=1, source_target_pairs={{0,32},{32,0},{64,96},{96,64},{128,160},{160,128},{192,224},{224,1... | collective-permute-start | bytes 860168 | tf_op jit(solution)/shard_map/ppermute | solution.py:20
  18.4 35.4 %collective-permute-done.4 = bf16[160,896]{1,0:T(8,128)(2,1)S(1)} collective-permute-done((bf16[160,896]{1,0:T(8,128)(2,1)S(1)}, bf16[160,896]{1,0:T(8,128)(2,1)S(1)}, u32[]{:S(2)}, u32[]{:S(2)}) %collective-permute-start.4) | collective-permute-done | bytes 286752 | tf_op jit(solution)/shard_map/ppermute | solution.py:20
  53.8 1.6 convolution_convert_fusion.2
  55.4 5.8 %all-to-all-done = bf16[32,24,896]{2,1,0:T(8,128)(2,1)S(1)} async-done(((bf16[32,24,896]{2,1,0:T(8,128)(2,1)}), bf16[32,24,896]{2,1,0:T(8,128)(2,1)S(1)}, u32[]{:S(2)}, u32[]{:S(2)}) %all-to-all-start) | async-done | bytes 1376288 | tf_op jit(solution)/shard_map/all_to_all | solution.py:38
  61.2 4.7 %all-to-all-start.1 = ((bf16[32,24,896]{2,1,0:T(8,128)(2,1)}), bf16[32,24,896]{2,1,0:T(8,128)(2,1)}, u32[]{:S(2)}, u32[]{:S(2)}) async-start(bf16[32,24,896]{2,1,0:T(8,128)(2,1)} %bitcast.50), calls=%async_computation.1 | async-start | bytes 2752512 | tf_op jit(solution)/shard_map/all_to_all | solution.py:38
  66.0 2.1 convolution_convert_fusion.5.refs_0_
  68.1 1.3 collective-permute-start.1
  69.3 1.5 collective-permute-start
  70.8 30.0 %all-to-all-done.1 = bf16[32,24,896]{2,1,0:T(8,128)(2,1)} async-done(((bf16[32,24,896]{2,1,0:T(8,128)(2,1)}), bf16[32,24,896]{2,1,0:T(8,128)(2,1)}, u32[]{:S(2)}, u32[]{:S(2)}) %all-to-all-start.1) | async-done | bytes 1376288 | tf_op jit(solution)/shard_map/all_to_all | solution.py:38
  100.9 4.0 %convolution_convert_fusion.4.refs_2_ = bf16[640,896]{1,0:T(8,128)(2,1)} fusion(bf16[768,896]{1,0:T(8,128)(2,1)} %bitcast.7, s32[640]{0:T(1024)S(1)} %get-tuple-element.36, s32[640]{0:T(1024)S(1)} %get-tuple-element.37, s32[640]{0:T(1024)S(1)} %get-tuple-element.35, s32[640]{0:T(1024)S(1)} %get-tuple-element.38, pred[640]{0:T(1024)(128)(4,1)S(1)} %get-tuple-element.39, ...), kind=kOutput, calls=%fused_computation.7 | convolution fusion | flops 883834880 | bytes 2534656 | tf_op jit(solution)/shard_map/dot_general | solution.py:49
  104.9 1.2 collective-permute-start.6
  106.1 1.5 collective-permute-start.5
  109.3 2.7 collective-permute-start.3
  112.0 20.8 %collective-permute-done.6.refs_5_ = bf16[640,896]{1,0:T(8,128)(2,1)} collective-permute-done((bf16[640,896]{1,0:T(8,128)(2,1)}, bf16[640,896]{1,0:T(8,128)(2,1)}, u32[]{:S(2)}, u32[]{:S(2)}) %collective-permute-start.6) | collective-permute-done | bytes 1146912 | tf_op jit(solution)/shard_map/ppermute | solution.py:16
  132.8 1.3 slice.88
  134.2 1.1 slice.89
  135.3 2.9 collective-permute-start.8
  138.3 6.8 %collective-permute-done.2 = bf16[320,896]{1,0:T(8,128)(2,1)} collective-permute-done((bf16[320,896]{1,0:T(8,128)(2,1)}, bf16[320,896]{1,0:T(8,128)(2,1)}, u32[]{:S(2)}, u32[]{:S(2)}) %collective-permute-start.2) | collective-permute-done | bytes 573472 | tf_op jit(solution)/shard_map/ppermute | solution.py:16
  145.1 1.3 pad_maximum_fusion.refs_2_
  146.5 2.0 copy-done.1
  148.5 4.0 %shard_map.64 = (f32[640,256]{1,0:T(8,128)S(1)}, f32[640,256]{1,0:T(8,128)S(1)}) custom-call(s32[8]{0:T(128)S(1)} %pad_add_fusion.idx, bf16[640,896]{1,0:T(8,128)(2,1)S(1)} %convolution_convert_fusion.5.refs_0_, bf16[640,896]{1,0:T(8,128)(2,1)S(1)} %collective-permute-done.refs_1_, bf16[640,896]{1,0:T(8,128)(2,1)S(1)} %pad_maximum_fusion.refs_2_, ...), custom_call_target="tpu_custom_call" | custom-call | flops 2348810240 | bytes 20971520 | tf_op jit(solution)/shard_map/pallas_call | solution.py:112
  152.5 4.8 %collective-permute-done.7 = bf16[320,896]{1,0:T(8,128)(2,1)S(1)} collective-permute-done((bf16[320,896]{1,0:T(8,128)(2,1)S(1)}, bf16[320,896]{1,0:T(8,128)(2,1)S(1)}, u32[]{:S(2)}, u32[]{:S(2)}) %collective-permute-start.7) | collective-permute-done | bytes 573472 | tf_op jit(solution)/shard_map/ppermute | solution.py:16
  157.3 1.1 pad_maximum_fusion.1.refs_4_
  158.4 12.1 %shard_map.65 = (bf16[640,896]{1,0:T(8,128)(2,1)S(1)}, bf16[640,896]{1,0:T(8,128)(2,1)S(1)}, bf16[640,896]{1,0:T(8,128)(2,1)S(1)}, bf16[640,896]{1,0:T(8,128)(2,...) custom-call(s32[8]{0:T(128)S(1)} %pad_add_fusion.idx, ...), custom_call_target="tpu_custom_call" | custom-call | flops 4697620480 | bytes 31457280 | tf_op jit(solution)/shard_map/pallas_call | solution.py:133
  170.5 1.5 fusion.41
  172.0 1.0 collective-permute-start.13
  172.9 1.8 collective-permute-start.15
  174.8 11.6 %collective-permute-done.13 = bf16[320,896]{1,0:T(8,128)(2,1)S(1)} collective-permute-done((bf16[320,896]{1,0:T(8,128)(2,1)S(1)}, bf16[320,896]{1,0:T(8,128)(2,1)S(1)}, u32[]{:S(2)}, u32[]{:S(2)}) %collective-permute-start.13) | collective-permute-done | bytes 573472 | tf_op jit(solution)/shard_map/ppermute | solution.py:16
  187.1 2.7 collective-permute-start.16
  189.8 1.1 fusion.40
  190.9 21.7 %collective-permute-done.14 = bf16[640,896]{1,0:T(8,128)(2,1)S(1)} collective-permute-done((bf16[640,896]{1,0:T(8,128)(2,1)S(1)}, bf16[640,896]{1,0:T(8,128)(2,1)S(1)}, u32[]{:S(2)}, u32[]{:S(2)}) %collective-permute-start.14) | collective-permute-done | bytes 1146912 | tf_op jit(solution)/shard_map/ppermute | solution.py:16
  212.6 2.8 convolution_convert_fusion
  215.4 10.1 %all-to-all-start.3 = ((bf16[32,24,896]{2,1,0:T(8,128)(2,1)}), bf16[32,24,896]{2,1,0:T(8,128)(2,1)}, u32[]{:S(2)}, u32[]{:S(2)}) async-start(bf16[32,24,896]{2,1,0:T(8,128)(2,1)} %bitcast.48), calls=%async_computation.3 | async-start | bytes 2752512 | tf_op jit(solution)/shard_map/all_to_all | solution.py:38
  225.5 0.9 collective-permute-start.11
  226.5 1.2 add_convert_fusion.7
  228.5 11.5 %collective-permute-done.11 = bf16[320,896]{1,0:T(8,128)(2,1)S(1)} collective-permute-done((bf16[320,896]{1,0:T(8,128)(2,1)}, bf16[320,896]{1,0:T(8,128)(2,1)S(1)}, u32[]{:S(2)}, u32[]{:S(2)}) %collective-permute-start.11) | collective-permute-done | bytes 573472 | tf_op jit(solution)/shard_map/ppermute | solution.py:16
  240.3 2.5 collective-permute-start.12
  242.8 11.6 %collective-permute-done.10 = bf16[640,896]{1,0:T(8,128)(2,1)S(1)} collective-permute-done((bf16[640,896]{1,0:T(8,128)(2,1)S(1)}, bf16[640,896]{1,0:T(8,128)(2,1)S(1)}, u32[]{:S(2)}, u32[]{:S(2)}) %collective-permute-start.10) | collective-permute-done | bytes 1146912 | tf_op jit(solution)/shard_map/ppermute | solution.py:16
  254.4 12.0 %collective-permute-done.12 = bf16[640,896]{1,0:T(8,128)(2,1)S(1)} collective-permute-done((bf16[640,896]{1,0:T(8,128)(2,1)S(1)}, bf16[640,896]{1,0:T(8,128)(2,1)S(1)}, u32[]{:S(2)}, u32[]{:S(2)}) %collective-permute-start.12) | collective-permute-done | bytes 1146912 | tf_op jit(solution)/shard_map/ppermute | solution.py:16
  266.3 2.8 convolution_convert_fusion.1
  269.1 9.6 %all-to-all-start.2 = ((bf16[32,24,896]{2,1,0:T(8,128)(2,1)}), bf16[32,24,896]{2,1,0:T(8,128)(2,1)S(1)}, u32[]{:S(2)}, u32[]{:S(2)}) async-start(bf16[32,24,896]{2,1,0:T(8,128)(2,1)} %bitcast.9), calls=%async_computation.2 | async-start | bytes 2752512 | tf_op jit(solution)/shard_map/all_to_all | solution.py:38
  278.7 1.8 convolution_multiply_fusion
  280.6 1.8 fusion.2
  282.4 4.3 %collective-permute-start.17 = (bf16[160,896]{1,0:T(8,128)(2,1)S(1)}, bf16[160,896]{1,0:T(8,128)(2,1)S(1)}, u32[]{:S(2)}, u32[]{:S(2)}) collective-permute-start(bf16[160,896]{1,0:T(8,128)(2,1)S(1)} %fusion.2), channel_id=1, source_target_pairs={{0,32},{32,0},{64,96},{96,64},{128,160},{160,128},{192,224},{224,1... | collective-permute-start | bytes 860168 | tf_op jit(solution)/shard_map/ppermute | solution.py:20
  286.7 39.1 %all-to-all-done.2 = bf16[32,24,896]{2,1,0:T(8,128)(2,1)S(1)} async-done(((bf16[32,24,896]{2,1,0:T(8,128)(2,1)}), bf16[32,24,896]{2,1,0:T(8,128)(2,1)S(1)}, u32[]{:S(2)}, u32[]{:S(2)}) %all-to-all-start.2) | async-done | bytes 1376288 | tf_op jit(solution)/shard_map/all_to_all | solution.py:38
  326.3 1.2 add_convert_fusion.8
  (53 shorter events, 5.4 us)
Async XLA Ops:
  3.8 10.3 %copy-start.6 = (bf16[160,896]{1,0:T(8,128)(2,1)S(1)}, bf16[160,896]{1,0:T(8,128)(2,1)}, u32[]{:S(2)}) copy-start(bf16[160,896]{1,0:T(8,128)(2,1)} %param.6) | copy-start | bytes 860164
  3.8 57.4 %all-to-all-start = ((bf16[32,24,896]{2,1,0:T(8,128)(2,1)}), bf16[32,24,896]{2,1,0:T(8,128)(2,1)S(1)}, u32[]{:S(2)}, u32[]{:S(2)}) async-start(bf16[32,24,896]{2,1,0:T(8,128)(2,1)} %bitcast.51), calls=%async_computation | async-start | bytes 2752512 | tf_op jit(solution)/shard_map/all_to_all | solution.py:38
  14.1 39.7 %collective-permute-start.4 = (bf16[160,896]{1,0:T(8,128)(2,1)S(1)}, bf16[160,896]{1,0:T(8,128)(2,1)S(1)}, u32[]{:S(2)}, u32[]{:S(2)}) collective-permute-start(bf16[160,896]{1,0:T(8,128)(2,1)S(1)} %copy-done.6), channel_id=1, source_target_pairs={{0,32},{32,0},{64,96},{96,64},{128,160},{160,128},{192,224},{224,1... | collective-permute-start | bytes 860168 | tf_op jit(solution)/shard_map/ppermute | solution.py:20
  61.2 39.7 %all-to-all-start.1 = ((bf16[32,24,896]{2,1,0:T(8,128)(2,1)}), bf16[32,24,896]{2,1,0:T(8,128)(2,1)}, u32[]{:S(2)}, u32[]{:S(2)}) async-start(bf16[32,24,896]{2,1,0:T(8,128)(2,1)} %bitcast.50), calls=%async_computation.1 | async-start | bytes 2752512 | tf_op jit(solution)/shard_map/all_to_all | solution.py:38
  68.1 39.5 %collective-permute-start.1 = (bf16[640,896]{1,0:T(8,128)(2,1)S(1)}, bf16[640,896]{1,0:T(8,128)(2,1)S(1)}, u32[]{:S(2)}, u32[]{:S(2)}) collective-permute-start(bf16[640,896]{1,0:T(8,128)(2,1)S(1)} %convolution_convert_fusion.5.refs_0_), channel_id=1, source_target_pairs={{0,64},{32,96},{64,128},{96,160},{128,192},{160,224},{192,0},{224,... | collective-permute-start | bytes 3440648 | tf_op jit(solution)/shard_map/ppermute | solution.py:16
  69.3 39.1 %collective-permute-start = (bf16[640,896]{1,0:T(8,128)(2,1)S(1)}, bf16[640,896]{1,0:T(8,128)(2,1)S(1)}, u32[]{:S(2)}, u32[]{:S(2)}) collective-permute-start(bf16[640,896]{1,0:T(8,128)(2,1)S(1)} %convolution_convert_fusion.5.refs_0_), channel_id=1, source_target_pairs={{0,192},{32,224},{64,0},{96,32},{128,64},{160,96},{192,128},{224,1... | collective-permute-start | bytes 3440648 | tf_op jit(solution)/shard_map/ppermute | solution.py:16
  104.9 27.9 %collective-permute-start.6 = (bf16[640,896]{1,0:T(8,128)(2,1)}, bf16[640,896]{1,0:T(8,128)(2,1)}, u32[]{:S(2)}, u32[]{:S(2)}) collective-permute-start(bf16[640,896]{1,0:T(8,128)(2,1)} %convolution_convert_fusion.4.refs_2_), channel_id=1, source_target_pairs={{0,64},{32,96},{64,128},{96,160},{128,192},{160,224},{192,0},{224,... | collective-permute-start | bytes 3440648 | tf_op jit(solution)/shard_map/ppermute | solution.py:16
  106.1 28.1 %collective-permute-start.5 = (bf16[640,896]{1,0:T(8,128)(2,1)}, bf16[640,896]{1,0:T(8,128)(2,1)}, u32[]{:S(2)}, u32[]{:S(2)}) collective-permute-start(bf16[640,896]{1,0:T(8,128)(2,1)} %convolution_convert_fusion.4.refs_2_), channel_id=1, source_target_pairs={{0,192},{32,224},{64,0},{96,32},{128,64},{160,96},{192,128},{224,1... | collective-permute-start | bytes 3440648 | tf_op jit(solution)/shard_map/ppermute | solution.py:16
  108.4 36.7 %collective-permute-start.2 = (bf16[320,896]{1,0:T(8,128)(2,1)}, bf16[320,896]{1,0:T(8,128)(2,1)}, u32[]{:S(2)}, u32[]{:S(2)}) collective-permute-start(bf16[320,896]{1,0:T(8,128)(2,1)} %slice.86), channel_id=1, source_target_pairs={{0,64},{32,96},{64,128},{96,160},{128,192},{160,224},{192,0},{224,... | collective-permute-start | bytes 1720328 | tf_op jit(solution)/shard_map/ppermute | solution.py:16
  109.3 35.8 %collective-permute-start.3 = (bf16[320,896]{1,0:T(8,128)(2,1)}, bf16[320,896]{1,0:T(8,128)(2,1)}, u32[]{:S(2)}, u32[]{:S(2)}) collective-permute-start(bf16[320,896]{1,0:T(8,128)(2,1)} %slice.87), channel_id=1, source_target_pairs={{0,192},{32,224},{64,0},{96,32},{128,64},{160,96},{192,128},{224,1... | collective-permute-start | bytes 1720328 | tf_op jit(solution)/shard_map/ppermute | solution.py:16
  132.8 13.6 %copy-start = (bf16[1,7168,256]{2,1,0:T(8,128)(2,1)S(1)}, bf16[1,7168,256]{2,1,0:T(8,128)(2,1)}, u32[]{:S(2)}) copy-start(bf16[1,7168,256]{2,1,0:T(8,128)(2,1)} %param.9) | copy-start | bytes 11010052
  134.1 23.2 %collective-permute-start.7 = (bf16[320,896]{1,0:T(8,128)(2,1)S(1)}, bf16[320,896]{1,0:T(8,128)(2,1)S(1)}, u32[]{:S(2)}, u32[]{:S(2)}) collective-permute-start(bf16[320,896]{1,0:T(8,128)(2,1)S(1)} %slice.88), channel_id=1, source_target_pairs={{0,64},{32,96},{64,128},{96,160},{128,192},{160,224},{192,0},{224,... | collective-permute-start | bytes 1720328 | tf_op jit(solution)/shard_map/ppermute | solution.py:16
  135.3 22.0 %collective-permute-start.8 = (bf16[320,896]{1,0:T(8,128)(2,1)S(1)}, bf16[320,896]{1,0:T(8,128)(2,1)S(1)}, u32[]{:S(2)}, u32[]{:S(2)}) collective-permute-start(bf16[320,896]{1,0:T(8,128)(2,1)S(1)} %slice.89), channel_id=1, source_target_pairs={{0,192},{32,224},{64,0},{96,32},{128,64},{160,96},{192,128},{224,1... | collective-permute-start | bytes 1720328 | tf_op jit(solution)/shard_map/ppermute | solution.py:16
  146.4 2.0 copy-start.1
  170.5 4.3 %copy-start.3 = (bf16[640,896]{1,0:T(8,128)(2,1)S(1)}, bf16[640,896]{1,0:T(8,128)(2,1)}, u32[]{:S(2)}) copy-start(bf16[640,896]{1,0:T(8,128)(2,1)} %get-tuple-element.22) | copy-start | bytes 3440644
  170.5 4.3 %copy-start.2 = (bf16[640,896]{1,0:T(8,128)(2,1)S(1)}, bf16[640,896]{1,0:T(8,128)(2,1)}, u32[]{:S(2)}) copy-start(bf16[640,896]{1,0:T(8,128)(2,1)} %get-tuple-element.24) | copy-start | bytes 3440644
  172.0 14.5 %collective-permute-start.13 = (bf16[320,896]{1,0:T(8,128)(2,1)S(1)}, bf16[320,896]{1,0:T(8,128)(2,1)S(1)}, u32[]{:S(2)}, u32[]{:S(2)}) collective-permute-start(bf16[320,896]{1,0:T(8,128)(2,1)S(1)} %get-tuple-element.27), channel_id=1, source_target_pairs={{0,64},{32,96},{64,128},{96,160},{128,192},{160,224},{192,0},{224,... | collective-permute-start | bytes 1720328 | tf_op jit(solution)/shard_map/ppermute | solution.py:16
  172.9 13.8 %collective-permute-start.15 = (bf16[320,896]{1,0:T(8,128)(2,1)S(1)}, bf16[320,896]{1,0:T(8,128)(2,1)S(1)}, u32[]{:S(2)}, u32[]{:S(2)}) collective-permute-start(bf16[320,896]{1,0:T(8,128)(2,1)S(1)} %get-tuple-element.28), channel_id=1, source_target_pairs={{0,192},{32,224},{64,0},{96,32},{128,64},{160,96},{192,128},{224,1... | collective-permute-start | bytes 1720328 | tf_op jit(solution)/shard_map/ppermute | solution.py:16
  186.7 25.9 %collective-permute-start.14 = (bf16[640,896]{1,0:T(8,128)(2,1)S(1)}, bf16[640,896]{1,0:T(8,128)(2,1)S(1)}, u32[]{:S(2)}, u32[]{:S(2)}) collective-permute-start(bf16[640,896]{1,0:T(8,128)(2,1)S(1)} %pad_maximum_fusion.4), channel_id=1, source_target_pairs={{0,64},{32,96},{64,128},{96,160},{128,192},{160,224},{192,0},{224,... | collective-permute-start | bytes 3440648 | tf_op jit(solution)/shard_map/ppermute | solution.py:16
  187.0 25.5 %copy-start.5 = (bf16[640,896]{1,0:T(8,128)(2,1)S(1)}, bf16[640,896]{1,0:T(8,128)(2,1)}, u32[]{:S(2)}) copy-start(bf16[640,896]{1,0:T(8,128)(2,1)} %get-tuple-element.21) | copy-start | bytes 3440644
  187.1 25.5 %collective-permute-start.16 = (bf16[640,896]{1,0:T(8,128)(2,1)S(1)}, bf16[640,896]{1,0:T(8,128)(2,1)S(1)}, u32[]{:S(2)}, u32[]{:S(2)}) collective-permute-start(bf16[640,896]{1,0:T(8,128)(2,1)S(1)} %pad_maximum_fusion.5), channel_id=1, source_target_pairs={{0,192},{32,224},{64,0},{96,32},{128,64},{160,96},{192,128},{224,1... | collective-permute-start | bytes 3440648 | tf_op jit(solution)/shard_map/ppermute | solution.py:16
  190.9 35.6 %collective-permute-start.9 = (bf16[320,896]{1,0:T(8,128)(2,1)}, bf16[320,896]{1,0:T(8,128)(2,1)}, u32[]{:S(2)}, u32[]{:S(2)}) collective-permute-start(bf16[320,896]{1,0:T(8,128)(2,1)} %get-tuple-element.25), channel_id=1, source_target_pairs={{0,64},{32,96},{64,128},{96,160},{128,192},{160,224},{192,0},{224,... | collective-permute-start | bytes 1720328 | tf_op jit(solution)/shard_map/ppermute | solution.py:16
  215.4 53.8 %all-to-all-start.3 = ((bf16[32,24,896]{2,1,0:T(8,128)(2,1)}), bf16[32,24,896]{2,1,0:T(8,128)(2,1)}, u32[]{:S(2)}, u32[]{:S(2)}) async-start(bf16[32,24,896]{2,1,0:T(8,128)(2,1)} %bitcast.48), calls=%async_computation.3 | async-start | bytes 2752512 | tf_op jit(solution)/shard_map/all_to_all | solution.py:38
  225.5 14.5 %collective-permute-start.11 = (bf16[320,896]{1,0:T(8,128)(2,1)}, bf16[320,896]{1,0:T(8,128)(2,1)S(1)}, u32[]{:S(2)}, u32[]{:S(2)}) collective-permute-start(bf16[320,896]{1,0:T(8,128)(2,1)} %get-tuple-element.26), channel_id=1, source_target_pairs={{0,192},{32,224},{64,0},{96,32},{128,64},{160,96},{192,128},{224,1... | collective-permute-start | bytes 1720328 | tf_op jit(solution)/shard_map/ppermute | solution.py:16
  227.8 26.5 %collective-permute-start.10 = (bf16[640,896]{1,0:T(8,128)(2,1)S(1)}, bf16[640,896]{1,0:T(8,128)(2,1)S(1)}, u32[]{:S(2)}, u32[]{:S(2)}) collective-permute-start(bf16[640,896]{1,0:T(8,128)(2,1)S(1)} %pad_maximum_fusion.2), channel_id=1, source_target_pairs={{0,64},{32,96},{64,128},{96,160},{128,192},{160,224},{192,0},{224,... | collective-permute-start | bytes 3440648 | tf_op jit(solution)/shard_map/ppermute | solution.py:16
  240.3 26.0 %collective-permute-start.12 = (bf16[640,896]{1,0:T(8,128)(2,1)S(1)}, bf16[640,896]{1,0:T(8,128)(2,1)S(1)}, u32[]{:S(2)}, u32[]{:S(2)}) collective-permute-start(bf16[640,896]{1,0:T(8,128)(2,1)S(1)} %pad_maximum_fusion.3), channel_id=1, source_target_pairs={{0,192},{32,224},{64,0},{96,32},{128,64},{160,96},{192,128},{224,1... | collective-permute-start | bytes 3440648 | tf_op jit(solution)/shard_map/ppermute | solution.py:16
  269.1 9.6 %copy-start.4 = (f32[160,2]{0,1:T(2,128)S(1)}, f32[160,2]{0,1:T(2,128)}, u32[]{:S(2)}) copy-start(f32[160,2]{0,1:T(2,128)} %param.8) | copy-start | bytes 3844
  269.1 56.6 %all-to-all-start.2 = ((bf16[32,24,896]{2,1,0:T(8,128)(2,1)}), bf16[32,24,896]{2,1,0:T(8,128)(2,1)S(1)}, u32[]{:S(2)}, u32[]{:S(2)}) async-start(bf16[32,24,896]{2,1,0:T(8,128)(2,1)} %bitcast.9), calls=%async_computation.2 | async-start | bytes 2752512 | tf_op jit(solution)/shard_map/all_to_all | solution.py:38
  282.4 43.9 %collective-permute-start.17 = (bf16[160,896]{1,0:T(8,128)(2,1)S(1)}, bf16[160,896]{1,0:T(8,128)(2,1)S(1)}, u32[]{:S(2)}, u32[]{:S(2)}) collective-permute-start(bf16[160,896]{1,0:T(8,128)(2,1)S(1)} %fusion.2), channel_id=1, source_target_pairs={{0,32},{32,0},{64,96},{96,64},{128,160},{160,128},{192,224},{224,1... | collective-permute-start | bytes 860168 | tf_op jit(solution)/shard_map/ppermute | solution.py:20

commit v2 on v0

v2 whole, which is shorter than its diff:
```python
import functools

import jax
import jax.numpy as jnp
from jax import lax
from jax.experimental import pallas as pl
from jax.experimental.pallas import tpu as pltpu
from jax.sharding import PartitionSpec as P

CAP_PAIR = 20
PAD_PAIR = 24


def move(x, by):
    return lax.ppermute(x, "rep", [(i, (i + 2 * by) % 8) for i in range(8)])


def swap(x):
    return lax.ppermute(x, "rep", [(i, i ^ 1) for i in range(8)])


def place_rows(slot_ids, n_ep):
    flat = slot_ids.T.reshape(-1)
    count = flat.shape[0]
    onehot = (flat[:, None] == jnp.arange(2 * n_ep, dtype=jnp.int32)[None, :]).astype(jnp.bfloat16)
    before = jnp.tril(jnp.ones((count, count), jnp.bfloat16), -1)
    ahead = jnp.dot(before, onehot, preferred_element_type=jnp.float32)
    position = jnp.sum(ahead * onehot.astype(jnp.float32), axis=1).astype(jnp.int32)
    odd = flat % 2
    expert = (flat // 2 - odd + n_ep) % n_ep
    row = expert * PAD_PAIR + odd * (CAP_PAIR // 2) + position
    return row.reshape(2, -1)


def exchange(rows, n_ep):
    width = rows.shape[1]
    out = lax.all_to_all(rows.reshape(n_ep, PAD_PAIR, width), "ep", 0, 0, tiled=True)
    return out.reshape(n_ep * PAD_PAIR, width)


def compact_matrix(pairs):
    r = lax.broadcasted_iota(jnp.int32, (pairs * CAP_PAIR, pairs * PAD_PAIR), 0)
    c = lax.broadcasted_iota(jnp.int32, (pairs * CAP_PAIR, pairs * PAD_PAIR), 1)
    return (r // CAP_PAIR * PAD_PAIR + r % CAP_PAIR == c).astype(jnp.bfloat16)


def pick(matrix, rows):
    return jnp.dot(matrix, rows, preferred_element_type=jnp.float32).astype(jnp.bfloat16)


def after(value, *first):
    return lax.optimization_barrier((value, *first))[0]


def ends(top, bottom):
    return move(top, 1), move(bottom, -1)


def sides(top, bottom):
    return move(bottom, 1), move(top, -1)


def add(*terms):
    return sum(t.astype(jnp.float32) for t in terms).astype(jnp.bfloat16)


def mm(a, b):
    return jnp.dot(a, b, preferred_element_type=jnp.float32)


def gate_up(pieces, start, idx, xs, wg, wu):
    sums = [list(pair) if pair else None for pair in start]
    for (block, h), x in zip(pieces, xs):
        width = x.shape[1]
        rows = pl.ds(pl.multiple_of(idx[block] * width, width), width)
        new = [mm(x[...], wg[rows, :]), mm(x[...], wu[rows, :])]
        sums[h] = [s + n for s, n in zip(sums[h], new)] if sums[h] else new
    return sums


def first_kernel(pieces, idx, *refs):
    xs, (wg, wu, g_ref, u_ref) = refs[:-4], refs[-4:]
    half = g_ref.shape[0] // 2
    for h, (gate, up) in enumerate(gate_up(pieces, [None, None], idx, xs, wg, wu)):
        g_ref[h * half : (h + 1) * half, :] = gate
        u_ref[h * half : (h + 1) * half, :] = up


def more_kernel(pieces, idx, g_in, u_in, *refs):
    xs, (wg, wu, g_ref, u_ref) = refs[:-4], refs[-4:]
    half = g_ref.shape[0] // 2
    at = [slice(h * half, (h + 1) * half) for h in range(2)]
    sums = gate_up(pieces, [(g_in[a, :], u_in[a, :]) for a in at], idx, xs, wg, wu)
    for a, (gate, up) in zip(at, sums):
        g_ref[a, :] = gate
        u_ref[a, :] = up


def second_kernel(pieces, far, idx, g_in, u_in, *refs):
    xs, (wg, wu, wd, h_ref, *outs) = refs[: len(pieces)], refs[len(pieces) :]
    half, width = xs[0].shape
    at = [slice(h * half, (h + 1) * half) for h in range(2)]
    sums = gate_up(pieces, [(g_in[a, :], u_in[a, :]) for a in at], idx, xs, wg, wu)
    columns = pl.ds(pl.multiple_of(idx[far] * width, width), width)
    for a, (gate, up), out in zip(at, sums, outs):
        hidden = (gate / (1.0 + jnp.exp(-gate)) * up).astype(jnp.bfloat16)
        h_ref[a, :] = hidden
        out[...] = mm(hidden, wd[:, columns]).astype(jnp.bfloat16)


def third_kernel(order, idx, h_ref, wd, *outs):
    half, width = outs[0].shape
    for i, b in enumerate(order):
        columns = pl.ds(pl.multiple_of(idx[b] * width, width), width)
        for h in range(2):
            hidden = h_ref[h * half : (h + 1) * half, :]
            outs[2 * i + h][...] = mm(hidden, wd[:, columns]).astype(jnp.bfloat16)


def call(body, outs, flops, *args):
    smem = pl.BlockSpec(memory_space=pltpu.SMEM)
    vmem = pl.BlockSpec(memory_space=pltpu.VMEM)
    size = sum(a.size * a.dtype.itemsize for a in (*args[1:], *outs))
    return pl.pallas_call(
        body,
        in_specs=[smem] + [vmem] * (len(args) - 1),
        out_specs=[vmem] * len(outs),
        out_shape=outs,
        compiler_params=pltpu.CompilerParams(vmem_limit_bytes=16 * 2**20),
        cost_estimate=pl.CostEstimate(flops=flops, bytes_accessed=size, transcendentals=0),
    )(*args)


def shards(tokens, slot_ids, weights, w_gate, w_up, w_down):
    n_ep = lax.axis_size("ep")
    rep = lax.axis_index("rep")
    near = [(rep + 2 * d) & 7 for d in range(4)]
    idx = jnp.stack(near + [a ^ 1 for a in near]).astype(jnp.int32)
    w_gate, w_up, w_down = w_gate[0], w_up[0], w_down[0]

    row = place_rows(slot_ids, n_ep)
    slots = lax.broadcasted_iota(jnp.int32, (n_ep * PAD_PAIR, tokens.shape[0]), 0)
    pack = ((slots == row[0][None]) | (slots == row[1][None])).astype(jnp.bfloat16)
    compact = compact_matrix(n_ep // 2)
    middle = n_ep * PAD_PAIR // 2

    arrived = exchange(pick(pack, tokens), n_ep)
    top, bottom = pick(compact, arrived[:middle]), pick(compact, arrived[middle:])
    left_top, right_bottom = ends(top, bottom)
    swap_top = swap(top)
    far_top, far_bottom = move(left_top, 1), move(right_bottom, -1)
    swap_bottom = swap(after(bottom, left_top, right_bottom))
    left_bottom, right_top = sides(after(top, left_top), after(bottom, right_bottom))

    half, width = top.shape
    hidden = w_gate.shape[1]
    unit = 4 * half * width * hidden
    bf16 = lambda *shape: jax.ShapeDtypeStruct(shape, jnp.bfloat16)
    acc = [jax.ShapeDtypeStruct((2 * half, hidden), jnp.float32)] * 2
    own = {
        (0, 0): top,
        (0, 1): bottom,
        (1, 0): right_top,
        (1, 1): right_bottom,
        (2, 0): far_top,
        (2, 1): far_bottom,
        (3, 0): left_top,
        (3, 1): left_bottom,
    }

    sums = call(
        functools.partial(first_kernel, list(own)), acc, 8 * unit, idx, *own.values(), w_gate, w_up
    )

    top = after(swap_top, left_bottom, right_top)
    left_top, right_top = move(top, 1), move(top, -1)
    bottom = after(swap_bottom, *sums, left_top, right_top)
    far_top = move(left_top, 1)
    left_bottom, right_bottom = move(bottom, 1), move(bottom, -1)
    far_bottom = move(right_bottom, -1)
    other = {
        (4, 0): top,
        (4, 1): bottom,
        (5, 0): right_top,
        (5, 1): right_bottom,
        (7, 0): left_top,
    }
    last = {(6, 0): far_top, (6, 1): far_bottom, (7, 1): left_bottom}

    sums = call(
        functools.partial(more_kernel, list(other)),
        acc,
        5 * unit,
        idx,
        *sums,
        *other.values(),
        w_gate,
        w_up,
    )
    units, *far = call(
        functools.partial(second_kernel, list(last), 6),
        [bf16(2 * half, hidden), bf16(half, width), bf16(half, width)],
        4 * unit,
        idx,
        *sums,
        *last.values(),
        w_gate,
        w_up,
        w_down,
    )
    order = (5, 7, 4, 2, 1, 3, 0)
    rest = call(
        functools.partial(third_kernel, order),
        [bf16(half, width)] * 14,
        7 * unit // 2,
        idx,
        units,
        w_down,
    )
    terms = {b: (rest[2 * i], rest[2 * i + 1]) for i, b in enumerate(order)}
    terms[6] = far

    a0, a1, a2, a3 = [terms[b] for b in (4, 5, 6, 7)]
    h0, h1, h2, h3 = [terms[b] for b in (0, 1, 2, 3)]
    far_top, far_bottom = ends(*a2)
    left_bottom, right_top = sides(a3[0], a1[1])
    left_top = move(add(a1[0], far_top), 1)
    right_bottom = move(add(a3[1], far_bottom), -1)
    home_far = ends(after(h2[0], left_bottom), after(h2[1], right_top))
    came = [
        swap(add(a0[0], left_top, right_top)),
        swap(add(a0[1], left_bottom, right_bottom)),
    ]
    left_bottom, right_top = sides(after(h3[0], right_bottom), after(h1[1], left_top))
    left_top = move(add(h1[0], home_far[0]), 1)
    right_bottom = move(add(h3[1], home_far[1]), -1)
    home = [add(h0[0], left_top, right_top), add(h0[1], left_bottom, right_bottom)]
    spread = compact.T
    total = [pick(spread, add(h, c)) for h, c in zip(home, came)]
    back = exchange(jnp.concatenate(total, axis=0), n_ep)

    columns = lax.broadcasted_iota(jnp.int32, (tokens.shape[0], n_ep * PAD_PAIR), 1)
    out = sum(
        weights[:, k : k + 1] * mm((columns == row[k][:, None]).astype(jnp.bfloat16), back)
        for k in range(2)
    )
    return out.astype(jnp.bfloat16)


def solution(mesh):
    placed = (
        P("ep", "rep"),
        P("ep", None),
        P("ep", None),
        P("ep", None, "rep"),
        P("ep", None, "rep"),
        P("ep", "rep", None),
    )
    return jax.shard_map(
        shards, mesh=mesh, in_specs=placed, out_specs=P("ep", "rep"), check_vma=False
    )
```

time: 934 us -> 275 us (0.29)
  waiting for transfers between devices: 615 us -> 182 us
  local copies, waits for them, and re-layouts: 242 us -> 8.92 us
  starting transfers between devices: 20.6 us -> 61.5 us
  matrix products: 22 us -> 6.96 us
  between operations: 13.9 us -> 0.2 us
  Pallas kernels: 0 us -> 12.9 us
    all_to_all x2, waiting for transfers between devices: 345 us -> 69.5 us  [exchange(): lax.all_to_all(rows.reshape(n_ep, PAD_PAIR, width), 'ep', 0, 0, tiled=True)]
    unnamed x3 -> x0, waiting for transfers between devices: 189 us -> none
    ppermute x3 -> x28, waiting for transfers between devices: 0.01 us -> 113 us  [the longest x24 64.1 us: move(): return lax.ppermute(x, 'rep', [(i, (i + 2 * by) % 8) for i in range(8)])]
    slice x2 -> x3, local copies, waits for them, and re-layouts: 103 us -> 0.19 us  [the longest x1 0.11 us: shards(): arrived[middle:]]
    all_gather x1 -> x0, waiting for transfers between devices: 79.8 us -> none  [shards(): wide_tokens = lax.all_gather(tokens, 'rep', axis=1, tiled=True)]
    unnamed x19 -> x22, local copies, waits for them, and re-layouts: 55.2 us -> 7.84 us
    ppermute x3 -> x28, starting transfers between devices: 3.44 us -> 43.4 us  [the longest x24 29.8 us: move(): return lax.ppermute(x, 'rep', [(i, (i + 2 * by) % 8) for i in range(8)])]
    reshape x5 -> x1, local copies, waits for them, and re-layouts: 40.4 us -> 0.81 us  [place_rows(): flat = slot_ids.T.reshape(-1)]
  transfers between devices with their start and end apart: 7 -> 30, of which waited for: 4 -> 15; matrix products, arithmetic and copies ran while one was open for 15% -> 1% of each run, Pallas kernels for 0% -> 4%
where the time goes in v2:
time: 275 us
  waiting for transfers between devices  182 us (66%)
  starting transfers between devices  61.5 us (22%)
  Pallas kernels  12.9 us (5%)
  local copies, waits for them, and re-layouts  8.92 us (3%)
  matrix products  6.96 us (3%)
    all_to_all x2, waiting for transfers between devices, exchange(): lax.all_to_all(rows.reshape(n_ep, PAD_PAIR, width), 'ep', 0, 0, tiled=True)  69.5 us
    ppermute x24, waiting for transfers between devices, move(): return lax.ppermute(x, 'rep', [(i, (i + 2 * by) % 8) for i in range(8)])  64.1 us
    ppermute x4, waiting for transfers between devices, swap(): return lax.ppermute(x, 'rep', [(i, i ^ 1) for i in range(8)])  48.6 us
    ppermute x24, starting transfers between devices, move(): return lax.ppermute(x, 'rep', [(i, (i + 2 * by) % 8) for i in range(8)])  29.8 us
    all_to_all x2, starting transfers between devices, exchange(): lax.all_to_all(rows.reshape(n_ep, PAD_PAIR, width), 'ep', 0, 0, tiled=True)  18.1 us
    ppermute x4, starting transfers between devices, swap(): return lax.ppermute(x, 'rep', [(i, i ^ 1) for i in range(8)])  13.5 us
    pallas_call x4, Pallas kernels, call(): pl.pallas_call(body, in_specs=[smem] + [vmem] * (len(args) - 1), out_spec...  12.9 us
    unnamed x22, local copies, waits for them, and re-layouts  7.84 us
  transfers between devices with their start and end apart: 30, of which 15 were waited for; matrix products, arithmetic and copies ran while one was open for 1% of the time, Pallas kernels for 4%

profile of v2, /device:TPU:1, one launch (start us, length us, event | category | flops | bytes accessed | tf_op | source)
XLA Modules:
  0.0 275.0 jit_solution(12668629913967955652)
XLA Ops:
  1.2 1.7 convolution_convert_fusion
  2.9 10.2 %all-to-all-start = ((bf16[32,24,896]{2,1,0:T(8,128)(2,1)}), bf16[32,24,896]{2,1,0:T(8,128)(2,1)S(1)}, u32[]{:S(2)}, u32[]{:S(2)}) async-start(bf16[32,24,896]{2,1,0:T(8,128)(2,1)} %bitcast.10), calls=%async_computation | async-start | bytes 2752512 | tf_op jit(solution)/shard_map/all_to_all | solution.py:37
  13.1 34.7 %all-to-all-done = bf16[32,24,896]{2,1,0:T(8,128)(2,1)S(1)} async-done(((bf16[32,24,896]{2,1,0:T(8,128)(2,1)}), bf16[32,24,896]{2,1,0:T(8,128)(2,1)S(1)}, u32[]{:S(2)}, u32[]{:S(2)}) %all-to-all-start) | async-done | bytes 1376288 | tf_op jit(solution)/shard_map/all_to_all | solution.py:37
  48.7 1.3 collective-permute-start
  50.8 1.5 collective-permute-start.2
  52.3 4.2 %collective-permute-start.6 = (bf16[320,896]{1,0:T(8,128)(2,1)S(1)}, bf16[320,896]{1,0:T(8,128)(2,1)S(1)}, u32[]{:S(2)}, u32[]{:S(2)}) collective-permute-start(bf16[320,896]{1,0:T(8,128)(2,1)S(1)} %convolution_convert_fusion.4.refs_0_), channel_id=1, source_target_pairs={{0,32},{32,0},{64,96},{96,64},{128,160},{160,128},{192,224},{224,1... | collective-permute-start | bytes 1720328 | tf_op jit(solution)/shard_map/ppermute | solution.py:19
  56.5 7.6 %collective-permute-done.refs_6_ = bf16[320,896]{1,0:T(8,128)(2,1)S(1)} collective-permute-done((bf16[320,896]{1,0:T(8,128)(2,1)S(1)}, bf16[320,896]{1,0:T(8,128)(2,1)S(1)}, u32[]{:S(2)}, u32[]{:S(2)}) %collective-permute-start) | collective-permute-done | bytes 573472 | tf_op jit(solution)/shard_map/ppermute | solution.py:15
  64.2 1.4 collective-permute-start.1
  66.0 0.9 collective-permute-start.3
  66.9 1.8 collective-permute-start.4
  68.6 14.1 %collective-permute-done.6.refs_0_ = bf16[320,896]{1,0:T(8,128)(2,1)S(1)} collective-permute-done((bf16[320,896]{1,0:T(8,128)(2,1)S(1)}, bf16[320,896]{1,0:T(8,128)(2,1)S(1)}, u32[]{:S(2)}, u32[]{:S(2)}) %collective-permute-start.6) | collective-permute-done | bytes 573472 | tf_op jit(solution)/shard_map/ppermute | solution.py:19
  82.8 2.1 collective-permute-start.7
  86.6 2.7 collective-permute-start.9
  89.3 2.8 %collective-permute-done.3.refs_4_ = bf16[320,896]{1,0:T(8,128)(2,1)} collective-permute-done((bf16[320,896]{1,0:T(8,128)(2,1)S(1)}, bf16[320,896]{1,0:T(8,128)(2,1)}, u32[]{:S(2)}, u32[]{:S(2)}) %collective-permute-start.3) | collective-permute-done | bytes 573472 | tf_op jit(solution)/shard_map/ppermute | solution.py:15
  92.2 2.0 copy-done.1
  94.2 2.0 copy-done.3
  96.2 1.1 copy-done.7
  97.3 1.1 copy-done.9
  98.4 4.4 %shard_map.64 = (f32[640,256]{1,0:T(8,128)S(1)}, f32[640,256]{1,0:T(8,128)S(1)}) custom-call(s32[8]{0:T(128)S(1)} %stack.35.idx, bf16[320,896]{1,0:T(8,128)(2,1)S(1)} %convolution_convert_fusion.4.refs_0_, bf16[320,896]{1,0:T(8,128)(2,1)S(1)} %convolution_convert_fusion.3.refs_1_, bf16[320,896]{1,0:T(8,128)(2,1)S(1)} %copy-done.7, ...), custom_call_target="tpu_custom_call" | custom-call | flops 2348810240 | bytes 13238272 | tf_op jit(solution)/shard_map/pallas_call | solution.py:124
  102.8 6.7 %collective-permute-done.7.refs_1_ = bf16[320,896]{1,0:T(8,128)(2,1)S(1)} collective-permute-done((bf16[320,896]{1,0:T(8,128)(2,1)S(1)}, bf16[320,896]{1,0:T(8,128)(2,1)S(1)}, u32[]{:S(2)}, u32[]{:S(2)}) %collective-permute-start.7) | collective-permute-done | bytes 573472 | tf_op jit(solution)/shard_map/ppermute | solution.py:19
  109.6 1.3 collective-permute-start.10
  111.1 12.6 %collective-permute-done.10.refs_3_ = bf16[320,896]{1,0:T(8,128)(2,1)S(1)} collective-permute-done((bf16[320,896]{1,0:T(8,128)(2,1)S(1)}, bf16[320,896]{1,0:T(8,128)(2,1)S(1)}, u32[]{:S(2)}, u32[]{:S(2)}) %collective-permute-start.10) | collective-permute-done | bytes 573472 | tf_op jit(solution)/shard_map/ppermute | solution.py:15
  123.6 2.5 collective-permute-start.12
  126.1 3.3 %shard_map.65 = (f32[640,256]{1,0:T(8,128)S(1)}, f32[640,256]{1,0:T(8,128)S(1)}) custom-call(s32[8]{0:T(128)S(1)} %stack.35.idx, f32[640,256]{1,0:T(8,128)S(1)} %get-tuple-element.37.g_in, f32[640,256]{1,0:T(8,128)S(1)} %get-tuple-element.38.u_in, bf16[320,896]{1,0:T(8,128)(2,1)S(1)} %collective-permute-done.6.refs_0_, ...), custom_call_target="tpu_custom_call" | custom-call | flops 1468006400 | bytes 12828672 | tf_op jit(solution)/shard_map/pallas_call | solution.py:124
  129.4 8.7 %collective-permute-done.11.refs_0_ = bf16[320,896]{1,0:T(8,128)(2,1)S(1)} collective-permute-done((bf16[320,896]{1,0:T(8,128)(2,1)}, bf16[320,896]{1,0:T(8,128)(2,1)S(1)}, u32[]{:S(2)}, u32[]{:S(2)}) %collective-permute-start.11) | collective-permute-done | bytes 573472 | tf_op jit(solution)/shard_map/ppermute | solution.py:15
  138.1 2.1 shard_map.66
  140.2 2.4 collective-permute-start.17
  142.6 3.1 %shard_map.67 = (bf16[320,896]{1,0:T(8,128)(2,1)S(1)}, bf16[320,896]{1,0:T(8,128)(2,1)S(1)}, bf16[320,896]{1,0:T(8,128)(2,1)S(1)}, bf16[320,896]{1,0:T(8,128)(2,...) custom-call(s32[8]{0:T(128)S(1)} %stack.35.idx, ...), custom_call_target="tpu_custom_call" | custom-call | flops 1027604480 | bytes 12025856 | tf_op jit(solution)/shard_map/pallas_call | solution.py:124
  145.9 1.4 collective-permute-start.20
  147.3 5.8 %collective-permute-done.17 = bf16[320,896]{1,0:T(8,128)(2,1)S(1)} collective-permute-done((bf16[320,896]{1,0:T(8,128)(2,1)S(1)}, bf16[320,896]{1,0:T(8,128)(2,1)S(1)}, u32[]{:S(2)}, u32[]{:S(2)}) %collective-permute-start.17) | collective-permute-done | bytes 573472 | tf_op jit(solution)/shard_map/ppermute | solution.py:15
  153.2 3.1 %collective-permute-start.18 = (bf16[320,896]{1,0:T(8,128)(2,1)S(1)}, bf16[320,896]{1,0:T(8,128)(2,1)S(1)}, u32[]{:S(2)}, u32[]{:S(2)}) collective-permute-start(bf16[320,896]{1,0:T(8,128)(2,1)S(1)} %add_convert_fusion.8), channel_id=1, source_target_pairs={{0,192},{32,224},{64,0},{96,32},{128,64},{160,96},{192,128},{224,1... | collective-permute-start | bytes 1720328 | tf_op jit(solution)/shard_map/ppermute | solution.py:15
  156.3 9.1 %collective-permute-done.22 = bf16[320,896]{1,0:T(8,128)(2,1)S(1)} collective-permute-done((bf16[320,896]{1,0:T(8,128)(2,1)S(1)}, bf16[320,896]{1,0:T(8,128)(2,1)S(1)}, u32[]{:S(2)}, u32[]{:S(2)}) %collective-permute-start.22) | collective-permute-done | bytes 573472 | tf_op jit(solution)/shard_map/ppermute | solution.py:15
  165.4 3.0 %collective-permute-start.25 = (bf16[320,896]{1,0:T(8,128)(2,1)S(1)}, bf16[320,896]{1,0:T(8,128)(2,1)S(1)}, u32[]{:S(2)}, u32[]{:S(2)}) collective-permute-start(bf16[320,896]{1,0:T(8,128)(2,1)S(1)} %get-tuple-element.63), channel_id=1, source_target_pairs={{0,192},{32,224},{64,0},{96,32},{128,64},{160,96},{192,128},{224,1... | collective-permute-start | bytes 1720328 | tf_op jit(solution)/shard_map/ppermute | solution.py:15
  168.6 2.8 %collective-permute-done.14 = bf16[320,896]{1,0:T(8,128)(2,1)S(1)} collective-permute-done((bf16[320,896]{1,0:T(8,128)(2,1)S(1)}, bf16[320,896]{1,0:T(8,128)(2,1)S(1)}, u32[]{:S(2)}, u32[]{:S(2)}) %collective-permute-start.14) | collective-permute-done | bytes 573472 | tf_op jit(solution)/shard_map/ppermute | solution.py:15
  171.4 6.3 %collective-permute-done.18 = bf16[320,896]{1,0:T(8,128)(2,1)S(1)} collective-permute-done((bf16[320,896]{1,0:T(8,128)(2,1)S(1)}, bf16[320,896]{1,0:T(8,128)(2,1)S(1)}, u32[]{:S(2)}, u32[]{:S(2)}) %collective-permute-start.18) | collective-permute-done | bytes 573472 | tf_op jit(solution)/shard_map/ppermute | solution.py:15
  177.9 3.6 %collective-permute-start.27 = (bf16[320,896]{1,0:T(8,128)(2,1)S(1)}, bf16[320,896]{1,0:T(8,128)(2,1)S(1)}, u32[]{:S(2)}, u32[]{:S(2)}) collective-permute-start(bf16[320,896]{1,0:T(8,128)(2,1)S(1)} %add_convert_fusion.1), channel_id=1, source_target_pairs={{0,32},{32,0},{64,96},{96,64},{128,160},{160,128},{192,224},{224,1... | collective-permute-start | bytes 1720328 | tf_op jit(solution)/shard_map/ppermute | solution.py:19
  181.5 8.5 %collective-permute-done.25 = bf16[320,896]{1,0:T(8,128)(2,1)S(1)} collective-permute-done((bf16[320,896]{1,0:T(8,128)(2,1)S(1)}, bf16[320,896]{1,0:T(8,128)(2,1)S(1)}, u32[]{:S(2)}, u32[]{:S(2)}) %collective-permute-start.25) | collective-permute-done | bytes 573472 | tf_op jit(solution)/shard_map/ppermute | solution.py:15
  190.1 3.1 %collective-permute-start.26 = (bf16[320,896]{1,0:T(8,128)(2,1)S(1)}, bf16[320,896]{1,0:T(8,128)(2,1)S(1)}, u32[]{:S(2)}, u32[]{:S(2)}) collective-permute-start(bf16[320,896]{1,0:T(8,128)(2,1)S(1)} %add_convert_fusion.3), channel_id=1, source_target_pairs={{0,192},{32,224},{64,0},{96,32},{128,64},{160,96},{192,128},{224,1... | collective-permute-start | bytes 1720328 | tf_op jit(solution)/shard_map/ppermute | solution.py:15
  193.4 3.6 %collective-permute-start.23 = (bf16[320,896]{1,0:T(8,128)(2,1)S(1)}, bf16[320,896]{1,0:T(8,128)(2,1)S(1)}, u32[]{:S(2)}, u32[]{:S(2)}) collective-permute-start(bf16[320,896]{1,0:T(8,128)(2,1)S(1)} %add_convert_fusion.5), channel_id=1, source_target_pairs={{0,32},{32,0},{64,96},{96,64},{128,160},{160,128},{192,224},{224,1... | collective-permute-start | bytes 1720328 | tf_op jit(solution)/shard_map/ppermute | solution.py:19
  197.0 2.7 collective-permute-start.19
  199.8 15.3 %collective-permute-done.27 = bf16[320,896]{1,0:T(8,128)(2,1)S(1)} collective-permute-done((bf16[320,896]{1,0:T(8,128)(2,1)S(1)}, bf16[320,896]{1,0:T(8,128)(2,1)S(1)}, u32[]{:S(2)}, u32[]{:S(2)}) %collective-permute-start.27) | collective-permute-done | bytes 573472 | tf_op jit(solution)/shard_map/ppermute | solution.py:19
  215.1 0.9 convolution_convert_fusion.1
  216.1 12.4 %collective-permute-done.23 = bf16[320,896]{1,0:T(8,128)(2,1)S(1)} collective-permute-done((bf16[320,896]{1,0:T(8,128)(2,1)S(1)}, bf16[320,896]{1,0:T(8,128)(2,1)S(1)}, u32[]{:S(2)}, u32[]{:S(2)}) %collective-permute-start.23) | collective-permute-done | bytes 573472 | tf_op jit(solution)/shard_map/ppermute | solution.py:19
  228.5 0.9 convolution_convert_fusion.2
  229.4 1.2 pad_maximum_fusion
  230.7 7.9 %all-to-all-start.1 = ((bf16[32,24,896]{2,1,0:T(8,128)(2,1)}), bf16[32,24,896]{2,1,0:T(8,128)(2,1)S(1)}, u32[]{:S(2)}, u32[]{:S(2)}) async-start(bf16[32,24,896]{2,1,0:T(8,128)(2,1)} %bitcast.16), calls=%async_computation.1 | async-start | bytes 2752512 | tf_op jit(solution)/shard_map/all_to_all | solution.py:37
  238.6 34.8 %all-to-all-done.1 = bf16[32,24,896]{2,1,0:T(8,128)(2,1)S(1)} async-done(((bf16[32,24,896]{2,1,0:T(8,128)(2,1)}), bf16[32,24,896]{2,1,0:T(8,128)(2,1)S(1)}, u32[]{:S(2)}, u32[]{:S(2)}) %all-to-all-start.1) | async-done | bytes 1376288 | tf_op jit(solution)/shard_map/all_to_all | solution.py:37
  273.8 1.2 fusion.1
  (63 shorter events, 6.9 us)
Async XLA Ops:
  0.0 1.2 copy-start
  2.9 45.0 %all-to-all-start = ((bf16[32,24,896]{2,1,0:T(8,128)(2,1)}), bf16[32,24,896]{2,1,0:T(8,128)(2,1)S(1)}, u32[]{:S(2)}, u32[]{:S(2)}) async-start(bf16[32,24,896]{2,1,0:T(8,128)(2,1)} %bitcast.10), calls=%async_computation | async-start | bytes 2752512 | tf_op jit(solution)/shard_map/all_to_all | solution.py:37
  48.7 15.4 %collective-permute-start = (bf16[320,896]{1,0:T(8,128)(2,1)S(1)}, bf16[320,896]{1,0:T(8,128)(2,1)S(1)}, u32[]{:S(2)}, u32[]{:S(2)}) collective-permute-start(bf16[320,896]{1,0:T(8,128)(2,1)S(1)} %convolution_convert_fusion.4.refs_0_), channel_id=1, source_target_pairs={{0,64},{32,96},{64,128},{96,160},{128,192},{160,224},{192,0},{224,... | collective-permute-start | bytes 1720328 | tf_op jit(solution)/shard_map/ppermute | solution.py:15
  50.8 14.8 %collective-permute-start.2 = (bf16[320,896]{1,0:T(8,128)(2,1)S(1)}, bf16[320,896]{1,0:T(8,128)(2,1)}, u32[]{:S(2)}, u32[]{:S(2)}) collective-permute-start(bf16[320,896]{1,0:T(8,128)(2,1)S(1)} %convolution_convert_fusion.3.refs_1_), channel_id=1, source_target_pairs={{0,192},{32,224},{64,0},{96,32},{128,64},{160,96},{192,128},{224,1... | collective-permute-start | bytes 1720328 | tf_op jit(solution)/shard_map/ppermute | solution.py:15
  52.3 30.5 %collective-permute-start.6 = (bf16[320,896]{1,0:T(8,128)(2,1)S(1)}, bf16[320,896]{1,0:T(8,128)(2,1)S(1)}, u32[]{:S(2)}, u32[]{:S(2)}) collective-permute-start(bf16[320,896]{1,0:T(8,128)(2,1)S(1)} %convolution_convert_fusion.4.refs_0_), channel_id=1, source_target_pairs={{0,32},{32,0},{64,96},{96,64},{128,160},{160,128},{192,224},{224,1... | collective-permute-start | bytes 1720328 | tf_op jit(solution)/shard_map/ppermute | solution.py:19
  64.2 20.8 %collective-permute-start.1 = (bf16[320,896]{1,0:T(8,128)(2,1)S(1)}, bf16[320,896]{1,0:T(8,128)(2,1)S(1)}, u32[]{:S(2)}, u32[]{:S(2)}) collective-permute-start(bf16[320,896]{1,0:T(8,128)(2,1)S(1)} %convolution_convert_fusion.4.refs_0_), channel_id=1, source_target_pairs={{0,192},{32,224},{64,0},{96,32},{128,64},{160,96},{192,128},{224,1... | collective-permute-start | bytes 1720328 | tf_op jit(solution)/shard_map/ppermute | solution.py:15
  65.5 20.2 %collective-permute-start.5 = (bf16[320,896]{1,0:T(8,128)(2,1)S(1)}, bf16[320,896]{1,0:T(8,128)(2,1)S(1)}, u32[]{:S(2)}, u32[]{:S(2)}) collective-permute-start(bf16[320,896]{1,0:T(8,128)(2,1)S(1)} %convolution_convert_fusion.3.refs_1_), channel_id=1, source_target_pairs={{0,64},{32,96},{64,128},{96,160},{128,192},{160,224},{192,0},{224,... | collective-permute-start | bytes 1720328 | tf_op jit(solution)/shard_map/ppermute | solution.py:15
  66.0 26.2 %collective-permute-start.3 = (bf16[320,896]{1,0:T(8,128)(2,1)S(1)}, bf16[320,896]{1,0:T(8,128)(2,1)}, u32[]{:S(2)}, u32[]{:S(2)}) collective-permute-start(bf16[320,896]{1,0:T(8,128)(2,1)S(1)} %collective-permute-done.refs_6_), channel_id=1, source_target_pairs={{0,64},{32,96},{64,128},{96,160},{128,192},{160,224},{192,0},{224,... | collective-permute-start | bytes 1720328 | tf_op jit(solution)/shard_map/ppermute | solution.py:15
  66.9 25.3 %collective-permute-start.4 = (bf16[320,896]{1,0:T(8,128)(2,1)}, bf16[320,896]{1,0:T(8,128)(2,1)}, u32[]{:S(2)}, u32[]{:S(2)}) collective-permute-start(bf16[320,896]{1,0:T(8,128)(2,1)} %collective-permute-done.2.refs_3_), channel_id=1, source_target_pairs={{0,192},{32,224},{64,0},{96,32},{128,64},{160,96},{192,128},{224,1... | collective-permute-start | bytes 1720328 | tf_op jit(solution)/shard_map/ppermute | solution.py:15
  82.8 26.8 %collective-permute-start.7 = (bf16[320,896]{1,0:T(8,128)(2,1)S(1)}, bf16[320,896]{1,0:T(8,128)(2,1)S(1)}, u32[]{:S(2)}, u32[]{:S(2)}) collective-permute-start(bf16[320,896]{1,0:T(8,128)(2,1)S(1)} %convolution_convert_fusion.3.refs_1_), channel_id=1, source_target_pairs={{0,32},{32,0},{64,96},{96,64},{128,160},{160,128},{192,224},{224,1... | collective-permute-start | bytes 1720328 | tf_op jit(solution)/shard_map/ppermute | solution.py:19
  84.9 0.8 copy-start.6
  85.7 0.8 copy-start.8
  86.6 23.0 %collective-permute-start.8 = (bf16[320,896]{1,0:T(8,128)(2,1)S(1)}, bf16[320,896]{1,0:T(8,128)(2,1)}, u32[]{:S(2)}, u32[]{:S(2)}) collective-permute-start(bf16[320,896]{1,0:T(8,128)(2,1)S(1)} %collective-permute-done.6.refs_0_), channel_id=1, source_target_pairs={{0,64},{32,96},{64,128},{96,160},{128,192},{160,224},{192,0},{224,... | collective-permute-start | bytes 1720328 | tf_op jit(solution)/shard_map/ppermute | solution.py:15
  86.6 23.0 %collective-permute-start.9 = (bf16[320,896]{1,0:T(8,128)(2,1)S(1)}, bf16[320,896]{1,0:T(8,128)(2,1)}, u32[]{:S(2)}, u32[]{:S(2)}) collective-permute-start(bf16[320,896]{1,0:T(8,128)(2,1)S(1)} %collective-permute-done.6.refs_0_), channel_id=1, source_target_pairs={{0,192},{32,224},{64,0},{96,32},{128,64},{160,96},{192,128},{224,1... | collective-permute-start | bytes 1720328 | tf_op jit(solution)/shard_map/ppermute | solution.py:15
  92.2 2.0 copy-start.1
  94.2 2.0 copy-start.3
  96.2 1.1 copy-start.7
  97.3 1.1 copy-start.9
  98.4 27.8 %copy-start.2 = (bf16[1,7168,256]{2,1,0:T(8,128)(2,1)S(1)}, bf16[1,7168,256]{2,1,0:T(8,128)(2,1)}, u32[]{:S(2)}) copy-start(bf16[1,7168,256]{2,1,0:T(8,128)(2,1)} %param.9) | copy-start | bytes 11010052
  98.4 27.8 %copy-start.4 = (bf16[1,7168,256]{2,1,0:T(8,128)(2,1)S(1)}, bf16[1,7168,256]{2,1,0:T(8,128)(2,1)}, u32[]{:S(2)}) copy-start(bf16[1,7168,256]{2,1,0:T(8,128)(2,1)} %param.10) | copy-start | bytes 11010052
  109.6 14.1 %collective-permute-start.10 = (bf16[320,896]{1,0:T(8,128)(2,1)S(1)}, bf16[320,896]{1,0:T(8,128)(2,1)S(1)}, u32[]{:S(2)}, u32[]{:S(2)}) collective-permute-start(bf16[320,896]{1,0:T(8,128)(2,1)S(1)} %collective-permute-done.7.refs_1_), channel_id=1, source_target_pairs={{0,192},{32,224},{64,0},{96,32},{128,64},{160,96},{192,128},{224,1... | collective-permute-start | bytes 1720328 | tf_op jit(solution)/shard_map/ppermute | solution.py:15
  110.8 27.2 %collective-permute-start.13 = (bf16[320,896]{1,0:T(8,128)(2,1)S(1)}, bf16[320,896]{1,0:T(8,128)(2,1)S(1)}, u32[]{:S(2)}, u32[]{:S(2)}) collective-permute-start(bf16[320,896]{1,0:T(8,128)(2,1)S(1)} %collective-permute-done.7.refs_1_), channel_id=1, source_target_pairs={{0,64},{32,96},{64,128},{96,160},{128,192},{160,224},{192,0},{224,... | collective-permute-start | bytes 1720328 | tf_op jit(solution)/shard_map/ppermute | solution.py:15
  111.0 27.0 %collective-permute-start.11 = (bf16[320,896]{1,0:T(8,128)(2,1)}, bf16[320,896]{1,0:T(8,128)(2,1)S(1)}, u32[]{:S(2)}, u32[]{:S(2)}) collective-permute-start(bf16[320,896]{1,0:T(8,128)(2,1)} %collective-permute-done.8.refs_4_), channel_id=1, source_target_pairs={{0,64},{32,96},{64,128},{96,160},{128,192},{160,224},{192,0},{224,... | collective-permute-start | bytes 1720328 | tf_op jit(solution)/shard_map/ppermute | solution.py:15
  123.6 14.5 %collective-permute-start.12 = (bf16[320,896]{1,0:T(8,128)(2,1)S(1)}, bf16[320,896]{1,0:T(8,128)(2,1)S(1)}, u32[]{:S(2)}, u32[]{:S(2)}) collective-permute-start(bf16[320,896]{1,0:T(8,128)(2,1)S(1)} %collective-permute-done.10.refs_3_), channel_id=1, source_target_pairs={{0,192},{32,224},{64,0},{96,32},{128,64},{160,96},{192,128},{224,1... | collective-permute-start | bytes 1720328 | tf_op jit(solution)/shard_map/ppermute | solution.py:15
  126.1 12.0 %copy-start.5 = (bf16[1,256,7168]{2,1,0:T(8,128)(2,1)S(1)}, bf16[1,256,7168]{2,1,0:T(8,128)(2,1)}, u32[]{:S(2)}) copy-start(bf16[1,256,7168]{2,1,0:T(8,128)(2,1)} %param.11) | copy-start | bytes 11010052
  140.2 12.9 %collective-permute-start.17 = (bf16[320,896]{1,0:T(8,128)(2,1)S(1)}, bf16[320,896]{1,0:T(8,128)(2,1)S(1)}, u32[]{:S(2)}, u32[]{:S(2)}) collective-permute-start(bf16[320,896]{1,0:T(8,128)(2,1)S(1)} %get-tuple-element.52), channel_id=1, source_target_pairs={{0,192},{32,224},{64,0},{96,32},{128,64},{160,96},{192,128},{224,1... | collective-permute-start | bytes 1720328 | tf_op jit(solution)/shard_map/ppermute | solution.py:15
  145.8 19.6 %collective-permute-start.22 = (bf16[320,896]{1,0:T(8,128)(2,1)S(1)}, bf16[320,896]{1,0:T(8,128)(2,1)S(1)}, u32[]{:S(2)}, u32[]{:S(2)}) collective-permute-start(bf16[320,896]{1,0:T(8,128)(2,1)S(1)} %get-tuple-element.57), channel_id=1, source_target_pairs={{0,192},{32,224},{64,0},{96,32},{128,64},{160,96},{192,128},{224,1... | collective-permute-start | bytes 1720328 | tf_op jit(solution)/shard_map/ppermute | solution.py:15
  145.9 22.5 %collective-permute-start.20 = (bf16[320,896]{1,0:T(8,128)(2,1)S(1)}, bf16[320,896]{1,0:T(8,128)(2,1)S(1)}, u32[]{:S(2)}, u32[]{:S(2)}) collective-permute-start(bf16[320,896]{1,0:T(8,128)(2,1)S(1)} %get-tuple-element.56), channel_id=1, source_target_pairs={{0,64},{32,96},{64,128},{96,160},{128,192},{160,224},{192,0},{224,... | collective-permute-start | bytes 1720328 | tf_op jit(solution)/shard_map/ppermute | solution.py:15
  147.3 24.1 %collective-permute-start.14 = (bf16[320,896]{1,0:T(8,128)(2,1)S(1)}, bf16[320,896]{1,0:T(8,128)(2,1)S(1)}, u32[]{:S(2)}, u32[]{:S(2)}) collective-permute-start(bf16[320,896]{1,0:T(8,128)(2,1)S(1)} %get-tuple-element.48), channel_id=1, source_target_pairs={{0,64},{32,96},{64,128},{96,160},{128,192},{160,224},{192,0},{224,... | collective-permute-start | bytes 1720328 | tf_op jit(solution)/shard_map/ppermute | solution.py:15
  153.2 24.4 %collective-permute-start.18 = (bf16[320,896]{1,0:T(8,128)(2,1)S(1)}, bf16[320,896]{1,0:T(8,128)(2,1)S(1)}, u32[]{:S(2)}, u32[]{:S(2)}) collective-permute-start(bf16[320,896]{1,0:T(8,128)(2,1)S(1)} %add_convert_fusion.8), channel_id=1, source_target_pairs={{0,192},{32,224},{64,0},{96,32},{128,64},{160,96},{192,128},{224,1... | collective-permute-start | bytes 1720328 | tf_op jit(solution)/shard_map/ppermute | solution.py:15
  165.4 24.6 %collective-permute-start.25 = (bf16[320,896]{1,0:T(8,128)(2,1)S(1)}, bf16[320,896]{1,0:T(8,128)(2,1)S(1)}, u32[]{:S(2)}, u32[]{:S(2)}) collective-permute-start(bf16[320,896]{1,0:T(8,128)(2,1)S(1)} %get-tuple-element.63), channel_id=1, source_target_pairs={{0,192},{32,224},{64,0},{96,32},{128,64},{160,96},{192,128},{224,1... | collective-permute-start | bytes 1720328 | tf_op jit(solution)/shard_map/ppermute | solution.py:15
  168.5 24.7 %collective-permute-start.21 = (bf16[320,896]{1,0:T(8,128)(2,1)S(1)}, bf16[320,896]{1,0:T(8,128)(2,1)S(1)}, u32[]{:S(2)}, u32[]{:S(2)}) collective-permute-start(bf16[320,896]{1,0:T(8,128)(2,1)S(1)} %add_convert_fusion.6), channel_id=1, source_target_pairs={{0,64},{32,96},{64,128},{96,160},{128,192},{160,224},{192,0},{224,... | collective-permute-start | bytes 1720328 | tf_op jit(solution)/shard_map/ppermute | solution.py:15
  171.4 25.6 %collective-permute-start.15 = (bf16[320,896]{1,0:T(8,128)(2,1)S(1)}, bf16[320,896]{1,0:T(8,128)(2,1)S(1)}, u32[]{:S(2)}, u32[]{:S(2)}) collective-permute-start(bf16[320,896]{1,0:T(8,128)(2,1)S(1)} %get-tuple-element.49), channel_id=1, source_target_pairs={{0,64},{32,96},{64,128},{96,160},{128,192},{160,224},{192,0},{224,... | collective-permute-start | bytes 1720328 | tf_op jit(solution)/shard_map/ppermute | solution.py:15
  177.9 37.2 %collective-permute-start.27 = (bf16[320,896]{1,0:T(8,128)(2,1)S(1)}, bf16[320,896]{1,0:T(8,128)(2,1)S(1)}, u32[]{:S(2)}, u32[]{:S(2)}) collective-permute-start(bf16[320,896]{1,0:T(8,128)(2,1)S(1)} %add_convert_fusion.1), channel_id=1, source_target_pairs={{0,32},{32,0},{64,96},{96,64},{128,160},{160,128},{192,224},{224,1... | collective-permute-start | bytes 1720328 | tf_op jit(solution)/shard_map/ppermute | solution.py:19
  190.1 25.0 %collective-permute-start.26 = (bf16[320,896]{1,0:T(8,128)(2,1)S(1)}, bf16[320,896]{1,0:T(8,128)(2,1)S(1)}, u32[]{:S(2)}, u32[]{:S(2)}) collective-permute-start(bf16[320,896]{1,0:T(8,128)(2,1)S(1)} %add_convert_fusion.3), channel_id=1, source_target_pairs={{0,192},{32,224},{64,0},{96,32},{128,64},{160,96},{192,128},{224,1... | collective-permute-start | bytes 1720328 | tf_op jit(solution)/shard_map/ppermute | solution.py:15
  193.2 22.0 %collective-permute-start.24 = (bf16[320,896]{1,0:T(8,128)(2,1)S(1)}, bf16[320,896]{1,0:T(8,128)(2,1)S(1)}, u32[]{:S(2)}, u32[]{:S(2)}) collective-permute-start(bf16[320,896]{1,0:T(8,128)(2,1)S(1)} %get-tuple-element.60), channel_id=1, source_target_pairs={{0,64},{32,96},{64,128},{96,160},{128,192},{160,224},{192,0},{224,... | collective-permute-start | bytes 1720328 | tf_op jit(solution)/shard_map/ppermute | solution.py:15
  193.4 35.1 %collective-permute-start.23 = (bf16[320,896]{1,0:T(8,128)(2,1)S(1)}, bf16[320,896]{1,0:T(8,128)(2,1)S(1)}, u32[]{:S(2)}, u32[]{:S(2)}) collective-permute-start(bf16[320,896]{1,0:T(8,128)(2,1)S(1)} %add_convert_fusion.5), channel_id=1, source_target_pairs={{0,32},{32,0},{64,96},{96,64},{128,160},{160,128},{192,224},{224,1... | collective-permute-start | bytes 1720328 | tf_op jit(solution)/shard_map/ppermute | solution.py:19
  197.0 31.5 %collective-permute-start.19 = (bf16[320,896]{1,0:T(8,128)(2,1)S(1)}, bf16[320,896]{1,0:T(8,128)(2,1)S(1)}, u32[]{:S(2)}, u32[]{:S(2)}) collective-permute-start(bf16[320,896]{1,0:T(8,128)(2,1)S(1)} %get-tuple-element.53), channel_id=1, source_target_pairs={{0,192},{32,224},{64,0},{96,32},{128,64},{160,96},{192,128},{224,1... | collective-permute-start | bytes 1720328 | tf_op jit(solution)/shard_map/ppermute | solution.py:15
  215.1 13.4 %collective-permute-start.16 = (bf16[320,896]{1,0:T(8,128)(2,1)S(1)}, bf16[320,896]{1,0:T(8,128)(2,1)S(1)}, u32[]{:S(2)}, u32[]{:S(2)}) collective-permute-start(bf16[320,896]{1,0:T(8,128)(2,1)S(1)} %add_convert_fusion.9), channel_id=1, source_target_pairs={{0,64},{32,96},{64,128},{96,160},{128,192},{160,224},{192,0},{224,... | collective-permute-start | bytes 1720328 | tf_op jit(solution)/shard_map/ppermute | solution.py:15
  230.7 7.9 %copy-start.10 = (f32[160,2]{0,1:T(2,128)S(1)}, f32[160,2]{0,1:T(2,128)}, u32[]{:S(2)}) copy-start(f32[160,2]{0,1:T(2,128)} %param.8) | copy-start | bytes 3844
  230.7 42.7 %all-to-all-start.1 = ((bf16[32,24,896]{2,1,0:T(8,128)(2,1)}), bf16[32,24,896]{2,1,0:T(8,128)(2,1)S(1)}, u32[]{:S(2)}, u32[]{:S(2)}) async-start(bf16[32,24,896]{2,1,0:T(8,128)(2,1)} %bitcast.16), calls=%async_computation.1 | async-start | bytes 2752512 | tf_op jit(solution)/shard_map/all_to_all | solution.py:37
